TPU v7x, 32 devices: a whole 2x2x4 slice. The times are simulated.
32 devices in a mesh: dp: 8 (over z, x), tensor: 4 (over y, core).
Axes of the slice: x: 2, y: 2, z: 4, core: 2. Of those that a mesh axis runs over, the one named last changes fastest.
Arguments:
- inputs: bfloat16 [1024, 16, 1024], P('tensor', 'dp'), may hold values from -6 to 6
- lengths: int32 [16], P('dp'), may hold values from 256 to 1024, as said below
- query_weight: bfloat16 [1024, 1024], P('dp', 'tensor'), may hold values from -0.1875 to 0.1875
- key_value_weight: bfloat16 [1024, 2, 512], P('dp', None, 'tensor'), may hold values from -0.1875 to 0.1875
- output_weight: bfloat16 [1024, 1024], P('tensor', 'dp'), may hold values from -3 to 3
- inner_weight: bfloat16 [1024, 2, 4608], P('dp', None, 'tensor'), may hold values from -0.1875 to 0.1875
- down_weight: bfloat16 [4608, 1024], P('tensor', 'dp'), may hold values from -0.09375 to 0.09375
- mixer_gain: float32 [1024], replicated, may hold values from 0.5 to 1.5
- query_gain: float32 [64], replicated, may hold values from 0.5 to 1.5
- key_gain: float32 [64], replicated, may hold values from 0.5 to 1.5
- dense_gain: float32 [1024], replicated, may hold values from 0.5 to 1.5
- cotangent: bfloat16 [1024, 16, 1024], P('tensor', 'dp'), may hold values from -6 to 6
Outputs:
- block_out: bfloat16 [1024, 16, 1024], P('tensor', 'dp')
- input_gradient: float32 [1024, 16, 1024], P('tensor', 'dp')
- query_gradient: float32 [1024, 1024], P('dp', 'tensor')
- pair_gradient: float32 [1024, 2, 512], P('dp', None, 'tensor')
- output_gradient: float32 [1024, 1024], P('tensor', 'dp')
- inner_gradient: float32 [1024, 2, 4608], P('dp', None, 'tensor')
- down_gradient: float32 [4608, 1024], P('tensor', 'dp')
- mixer_gain_gradient: float32 [1024], replicated
- query_gain_gradient: float32 [64], replicated
- key_gain_gradient: float32 [64], replicated
- dense_gain_gradient: float32 [1024], replicated
Inputs may be any that keep to these rules, and one draw needn't show every extreme that they name: `lengths`: among the 2 slots of each index of dp at least one has length 1024.
All inputs are finite; a program needn't handle non-finite values.
Results may differ from a plain program's by a relative error of at most 0.015.
Values may be sent and summed in bfloat16 or wider, within the bound.
A program may use at most 192 MiB of HBM per device.

v0:
```python
import jax
import jax.numpy as jnp
from jax import lax
from jax.sharding import PartitionSpec as P

EPS = 1e-05
THETA = 1000000.0


def norm_rows(values, gain):
    factor = lax.rsqrt(jnp.mean(values * values, axis=-1, keepdims=True) + EPS)
    return (values * factor * gain, factor)


def norm_back(values, factor, gain, upstream):
    weighted = upstream * gain
    inner = jnp.mean(values * weighted, axis=-1, keepdims=True)
    return factor * weighted - values * factor * factor * factor * inner


def tables(combined_length, head_width):
    half = head_width // 2
    freqs = THETA ** (-jnp.arange(half, dtype=jnp.float32) * 2.0 / head_width)
    angles = jnp.arange(combined_length, dtype=jnp.float32)[:, None] * freqs[None, :]
    return (jnp.cos(angles)[:, None, None, :], jnp.sin(angles)[:, None, None, :])


def rotate(values, cosines, sines):
    half = values.shape[-1] // 2
    first = values[..., :half]
    second = values[..., half:]
    return jnp.concatenate(
        [first * cosines - second * sines, second * cosines + first * sines], axis=-1
    )


def allowed_mask(start, row_count, key_pos, length):
    query_pos = start + jnp.arange(row_count, dtype=jnp.int32)
    return (key_pos[None, :] <= query_pos[:, None]) & (key_pos[None, :] < length)


def attend_forward(query_rows, keys, values, length):
    combined_length = query_rows.shape[0]
    row_count = min(512, combined_length)
    key_pos = jnp.arange(combined_length, dtype=jnp.int32)
    factor = query_rows.shape[-1] ** (-0.5)

    def step(carry, start):
        token_rows = lax.dynamic_slice_in_dim(query_rows, start, row_count, 0)
        scores = (
            jnp.einsum("qhgd,khd->hgqk", token_rows, keys, preferred_element_type=jnp.float32)
            * factor
        )
        scores = jnp.where(allowed_mask(start, row_count, key_pos, length), scores, -1e30)
        highest = jnp.max(scores, axis=-1, keepdims=True)
        weights = jnp.exp(scores - highest)
        summed = jnp.sum(weights, axis=-1, keepdims=True)
        probs = (weights / summed).astype(jnp.bfloat16)
        result = jnp.einsum("hgqk,khd->qhgd", probs, values, preferred_element_type=jnp.float32)
        return (carry, (result.astype(jnp.bfloat16), (highest + jnp.log(summed))[..., 0]))

    starts = jnp.arange(combined_length // row_count) * row_count
    _, (results, logsums) = lax.scan(step, 0, starts)
    return (results.reshape(query_rows.shape), logsums)


def attend_backward(query_rows, keys, values, length, logsums, grad_result):
    combined_length = query_rows.shape[0]
    row_count = min(512, combined_length)
    key_pos = jnp.arange(combined_length, dtype=jnp.int32)
    factor = query_rows.shape[-1] ** (-0.5)

    def step(carry, item):
        grad_keys, grad_values = carry
        start, log_rows = item
        token_rows = lax.dynamic_slice_in_dim(query_rows, start, row_count, 0)
        grad_rows = lax.dynamic_slice_in_dim(grad_result, start, row_count, 0)
        scores = (
            jnp.einsum("qhgd,khd->hgqk", token_rows, keys, preferred_element_type=jnp.float32)
            * factor
        )
        allowed = allowed_mask(start, row_count, key_pos, length)
        probs = jnp.where(
            allowed, jnp.exp(jnp.where(allowed, scores, -1e30) - log_rows[..., None]), 0.0
        )
        probs_low = probs.astype(jnp.bfloat16)
        grad_values = grad_values + jnp.einsum(
            "hgqk,qhgd->khd", probs_low, grad_rows, preferred_element_type=jnp.float32
        )
        grad_probs = jnp.einsum(
            "qhgd,khd->hgqk", grad_rows, values, preferred_element_type=jnp.float32
        )
        inner = jnp.sum(probs * grad_probs, axis=-1, keepdims=True)
        grad_scores = (probs * (grad_probs - inner)).astype(jnp.bfloat16)
        grad_queries = (
            jnp.einsum("hgqk,khd->qhgd", grad_scores, keys, preferred_element_type=jnp.float32)
            * factor
        )
        grad_keys = (
            grad_keys
            + jnp.einsum(
                "hgqk,qhgd->khd", grad_scores, token_rows, preferred_element_type=jnp.float32
            )
            * factor
        )
        return ((grad_keys, grad_values), grad_queries)

    starts = jnp.arange(combined_length // row_count) * row_count
    empty = jnp.zeros(keys.shape, jnp.float32)
    (grad_keys, grad_values), grad_queries = lax.scan(step, (empty, empty), (starts, logsums))
    return (grad_queries.reshape(query_rows.shape), grad_keys, grad_values)


def local(
    inputs,
    lengths,
    query_weight,
    key_value_weight,
    output_weight,
    inner_weight,
    down_weight,
    mixer_gain,
    query_gain,
    key_gain,
    dense_gain,
    cotangent,
):
    local_len, seq_count, width = inputs.shape
    full_len = local_len * lax.axis_size("tensor")
    head_width = query_gain.shape[0]
    query_cols = query_weight.shape[1]
    pair_cols = key_value_weight.shape[2]
    query_heads = query_cols // head_width
    pair_heads = pair_cols // head_width
    group_size = query_heads // pair_heads
    hidden_cols = inner_weight.shape[2]
    positions = lax.axis_index("tensor") * local_len + jnp.arange(local_len, dtype=jnp.int32)
    valid = (positions[:, None] < lengths[None, :])[:, :, None]
    cosines, sines = tables(full_len, head_width)
    inputs_full = inputs.astype(jnp.float32)
    normalized_rows, factor_first = norm_rows(inputs_full, mixer_gain)
    query_full, pair_full, output_full, inner_full, complete_down_weight = (
        lax.all_gather(query_weight, "dp", axis=0, tiled=True),
        lax.all_gather(key_value_weight, "dp", axis=0, tiled=True),
        lax.all_gather(output_weight, "dp", axis=1, tiled=True),
        lax.all_gather(inner_weight, "dp", axis=0, tiled=True),
        lax.all_gather(down_weight, "dp", axis=1, tiled=True),
    )
    joint_weight = jnp.concatenate([query_full, pair_full.reshape(width, 2 * pair_cols)], axis=1)
    inner_flat = inner_full.reshape(width, 2 * hidden_cols)
    weight_portion = lax.all_gather(
        normalized_rows.astype(jnp.bfloat16), "tensor", axis=0, tiled=True
    )
    projected = jnp.einsum(
        "lsd,de->lse", weight_portion, joint_weight, preferred_element_type=jnp.float32
    )
    normed_all = weight_portion
    queries_raw = projected[..., :query_cols].reshape(full_len, seq_count, query_heads, head_width)
    keys_raw = projected[..., query_cols : query_cols + pair_cols].reshape(
        full_len, seq_count, pair_heads, head_width
    )
    values_raw = projected[..., query_cols + pair_cols :].reshape(
        full_len, seq_count, pair_heads, head_width
    )
    queries_norm, factor_query = norm_rows(queries_raw, query_gain)
    keys_norm, factor_key = norm_rows(keys_raw, key_gain)
    query_rows = rotate(queries_norm, cosines, sines).astype(jnp.bfloat16)
    keys = rotate(keys_norm, cosines, sines).astype(jnp.bfloat16)
    values = values_raw.astype(jnp.bfloat16)
    query_groups = jnp.moveaxis(
        query_rows.reshape(full_len, seq_count, pair_heads, group_size, head_width), 1, 0
    )
    keys_seq = jnp.moveaxis(keys, 1, 0)
    values_seq = jnp.moveaxis(values, 1, 0)

    def forward_one(item):
        return attend_forward(item[0], item[1], item[2], item[3])

    attended_seq, logsums = lax.map(forward_one, (query_groups, keys_seq, values_seq, lengths))
    attended = jnp.moveaxis(attended_seq, 0, 1).reshape(full_len, seq_count, query_cols)
    token_rows = attended
    residual = inputs_full + lax.psum_scatter(
        jnp.einsum("lse,ed->lsd", token_rows, output_full, preferred_element_type=jnp.float32),
        "tensor",
        scatter_dimension=0,
        tiled=True,
    )
    dense_in, factor_dense = norm_rows(residual, dense_gain)
    weight_portion = lax.all_gather(dense_in.astype(jnp.bfloat16), "tensor", axis=0, tiled=True)
    gate_up = jnp.einsum(
        "lsd,de->lse", weight_portion, inner_flat, preferred_element_type=jnp.float32
    )
    dense_all = weight_portion
    gate = gate_up[..., :hidden_cols]
    up_part = gate_up[..., hidden_cols:]
    sig_gate = jax.nn.sigmoid(gate)
    hidden_state = (gate * sig_gate * up_part).astype(jnp.bfloat16)
    token_rows = hidden_state
    dense_sum = lax.psum_scatter(
        jnp.einsum(
            "pex,xa->pea", token_rows, complete_down_weight, preferred_element_type=jnp.float32
        ).astype(jnp.bfloat16),
        "tensor",
        scatter_dimension=0,
        tiled=True,
    ).astype(jnp.float32)
    block_out = jnp.where(valid, residual + dense_sum, 0.0).astype(jnp.bfloat16)
    upstream = jnp.where(valid, cotangent.astype(jnp.float32), 0.0)
    weight_portion = lax.all_gather(upstream.astype(jnp.bfloat16), "tensor", axis=0, tiled=True)
    hidden_state_gradient = jnp.einsum(
        "xnw,jw->xnj", weight_portion, complete_down_weight, preferred_element_type=jnp.float32
    )
    gathered_upstream_gradient = weight_portion
    down_gradient = jnp.einsum(
        "oxq,oxi->qi", hidden_state, gathered_upstream_gradient, preferred_element_type=jnp.float32
    )
    grad_gate = hidden_state_gradient * up_part * sig_gate * (1.0 + gate * (1.0 - sig_gate))
    grad_up = hidden_state_gradient * gate * sig_gate
    grad_gate_up = jnp.concatenate([grad_gate, grad_up], axis=-1).astype(jnp.bfloat16)
    inner_gradient = jnp.einsum(
        "lsd,lse->de", dense_all, grad_gate_up, preferred_element_type=jnp.float32
    ).reshape(width, 2, hidden_cols)
    token_rows = grad_gate_up
    grad_dense_in = lax.psum_scatter(
        jnp.einsum("lse,de->lsd", token_rows, inner_flat, preferred_element_type=jnp.float32),
        "tensor",
        scatter_dimension=0,
        tiled=True,
    )
    dense_gain_part = jnp.sum(grad_dense_in * residual * factor_dense, axis=(0, 1))
    grad_residual = upstream + norm_back(residual, factor_dense, dense_gain, grad_dense_in)
    grad_residual_low = grad_residual.astype(jnp.bfloat16)
    weight_portion = lax.all_gather(grad_residual_low, "tensor", axis=0, tiled=True)
    grad_attended_wide = jnp.einsum(
        "lsd,ed->lse", weight_portion, output_full, preferred_element_type=jnp.float32
    )
    grad_attended = grad_attended_wide.astype(jnp.bfloat16)
    output_gradient = jnp.einsum(
        "lse,lsd->ed", attended, weight_portion, preferred_element_type=jnp.float32
    )
    grad_attended_seq = jnp.moveaxis(
        grad_attended.reshape(full_len, seq_count, pair_heads, group_size, head_width), 1, 0
    )

    def backward_one(item):
        return attend_backward(item[0], item[1], item[2], item[3], item[4], item[5])

    grad_queries, grad_keys, grad_values = lax.map(
        backward_one, (query_groups, keys_seq, values_seq, lengths, logsums, grad_attended_seq)
    )
    grad_queries = jnp.moveaxis(grad_queries, 0, 1).reshape(
        full_len, seq_count, query_heads, head_width
    )
    grad_keys = jnp.moveaxis(grad_keys, 0, 1)
    grad_values = jnp.moveaxis(grad_values, 0, 1)
    turned_queries = rotate(grad_queries, cosines, -sines)
    turned_keys = rotate(grad_keys, cosines, -sines)
    query_gain_part = jnp.sum(turned_queries * queries_raw * factor_query, axis=(0, 1, 2))
    key_gain_part = jnp.sum(turned_keys * keys_raw * factor_key, axis=(0, 1, 2))
    grad_queries_raw = norm_back(queries_raw, factor_query, query_gain, turned_queries)
    grad_keys_raw = norm_back(keys_raw, factor_key, key_gain, turned_keys)
    grad_projected = jnp.concatenate(
        [
            grad_queries_raw.reshape(full_len, seq_count, query_cols),
            grad_keys_raw.reshape(full_len, seq_count, pair_cols),
            grad_values.reshape(full_len, seq_count, pair_cols),
        ],
        axis=-1,
    ).astype(jnp.bfloat16)
    joint_gradient = jnp.einsum(
        "lsd,lse->de", normed_all, grad_projected, preferred_element_type=jnp.float32
    )
    query_gradient = joint_gradient[:, :query_cols]
    pair_gradient = joint_gradient[:, query_cols:].reshape(width, 2, pair_cols)
    token_rows = grad_projected
    grad_normed = lax.psum_scatter(
        jnp.einsum(
            "lse,de->lsd", token_rows, joint_weight, preferred_element_type=jnp.float32
        ).astype(jnp.bfloat16),
        "tensor",
        scatter_dimension=0,
        tiled=True,
    ).astype(jnp.float32)
    mixer_gain_part = jnp.sum(grad_normed * inputs_full * factor_first, axis=(0, 1))
    input_gradient = grad_residual + norm_back(inputs_full, factor_first, mixer_gain, grad_normed)
    weight_sums = (
        lax.psum_scatter(query_gradient, "dp", scatter_dimension=0, tiled=True),
        lax.psum_scatter(pair_gradient, "dp", scatter_dimension=0, tiled=True),
        lax.psum_scatter(output_gradient, "dp", scatter_dimension=1, tiled=True),
        lax.psum_scatter(inner_gradient, "dp", scatter_dimension=0, tiled=True),
        lax.psum_scatter(down_gradient, "dp", scatter_dimension=1, tiled=True),
    )
    gain_sums = lax.psum(
        (mixer_gain_part, query_gain_part, key_gain_part, dense_gain_part), ("dp", "tensor")
    )
    return (
        block_out,
        input_gradient,
        weight_sums[0],
        weight_sums[1],
        weight_sums[2],
        weight_sums[3],
        weight_sums[4],
        gain_sums[0],
        gain_sums[1],
        gain_sums[2],
        gain_sums[3],
    )


def solution(mesh):
    return jax.shard_map(
        local,
        mesh=mesh,
        in_specs=(
            P("tensor", "dp", None),
            P("dp"),
            P("dp", "tensor"),
            P("dp", None, "tensor"),
            P("tensor", "dp"),
            P("dp", None, "tensor"),
            P("tensor", "dp"),
            P(),
            P(),
            P(),
            P(),
            P("tensor", "dp", None),
        ),
        out_specs=(
            P("tensor", "dp", None),
            P("tensor", "dp", None),
            P("dp", "tensor"),
            P("dp", None, "tensor"),
            P("tensor", "dp"),
            P("dp", None, "tensor"),
            P("tensor", "dp"),
            P(),
            P(),
            P(),
            P(),
        ),
        check_vma=False,
    )
```

profile of v0, /device:TPU:0, one launch (start us, length us, event | category | flops | bytes accessed | tf_op | source)
XLA Modules:
  0.0 1296.7 jit_solution(12835619208323913173)
XLA Ops:
  12.5 33.1 %all_gather.29 = bf16[1024,2,128]{2,1,0:T(2,128)(2,1)S(1)} all-gather(bf16[128,2,128]{2,1,0:T(2,128)(2,1)S(1)} %copy-done.27), channel_id=1, replica_groups=mesh['dp'=8,'tensor'=4] {'dp'}, dimensions={0}, use_global_device_ids=true | all-gather | bytes 589824 | tf_op jit(solution)/shard_map/all_gather | solution.py:144
  46.1 27.2 %all_gather.28 = bf16[1024,256]{0,1:T(8,128)(2,1)S(1)} all-gather(bf16[128,256]{0,1:T(8,128)(2,1)S(1)} %copy.79), channel_id=1, replica_groups=mesh['dp'=8,'tensor'=4] {'dp'}, dimensions={0}, use_global_device_ids=true | all-gather | bytes 589824 | tf_op jit(solution)/shard_map/all_gather | solution.py:143
  73.3 28.6 %all_gather.30 = bf16[256,1024]{1,0:T(8,128)(2,1)} all-gather(bf16[256,128]{1,0:T(8,128)(2,1)S(1)} %copy-done.28), channel_id=1, replica_groups=mesh['dp'=8,'tensor'=4] {'dp'}, dimensions={1}, use_global_device_ids=true | all-gather | bytes 589824 | tf_op jit(solution)/shard_map/all_gather | solution.py:145
  103.0 4.6 fusion.74
  111.2 56.7 %while.57 = (s32[]{:T(128)}, bf16[2,1024,2,2,64]{1,4,3,2,0:T(8,128)(2,1)}, f32[2,2,2,2,512]{4,3,2,1,0:T(2,128)S(1)}, bf16[2,1024,2,2,64]{1,4,3,2,0:T(8,128)(2,1)...) while((s32[]{:T(128)}, ...), condition=%wide.region_8.9_spmd, body=%wide.region_3.8_spmd.sunk | while | flops 563215872 | bytes 33659320 | solution.py:179
  112.8 23.6 %while.60 = (s32[]{:T(128)}, bf16[2,512,2,2,64]{1,4,3,2,0:T(8,128)(2,1)S(1)}, f32[2,2,2,512]{3,2,1,0:T(2,128)S(1)}, s32[2]{0:T(128)S(1)}, s32[]{:T(128)}, /*inde...) while((s32[]{:T(128)}, ...), condition=%wide.region_7.7_spmd.clone.clone, body=%wide.region_4.6_spmd.clone.clone.sunk | while | flops 563215872 | bytes 28383416 | solution.py:63
  121.5 3.1 fusion.143
  133.3 3.1 fusion.143
  141.1 23.6 %while.60 = (s32[]{:T(128)}, bf16[2,512,2,2,64]{1,4,3,2,0:T(8,128)(2,1)S(1)}, f32[2,2,2,512]{3,2,1,0:T(2,128)S(1)}, s32[2]{0:T(128)S(1)}, s32[]{:T(128)}, /*inde...) while((s32[]{:T(128)}, ...), condition=%wide.region_7.7_spmd.clone.clone, body=%wide.region_4.6_spmd.clone.clone.sunk | while | flops 563215872 | bytes 28383416 | solution.py:63
  149.8 3.1 fusion.143
  161.6 3.1 fusion.143
  167.8 6.5 fusion.76
  175.0 69.3 %reduce-scatter.8.cloned.1.call-done = f32[256,2,1024]{2,0,1:T(8,128)} async-done(((f32[1024,2,1024]{2,0,1:T(8,128)}), f32[256,2,1024]{2,0,1:T(8,128)}) %reduce-scatter.8.cloned.1.call-update) | async-done | bytes 2097168 | tf_op jit(solution)/shard_map/reduce_scatter | solution.py:182
  254.5 11.2 reshape.287
  265.7 23.5 %all-gather.9.cloned.1.call-done = bf16[1024,2,1024]{2,0,1:T(8,128)(2,1)} async-done(((bf16[256,2,1024]{2,0,1:T(8,128)(2,1)}), bf16[1024,2,1024]{2,0,1:T(8,128)(2,1)}) %all-gather.9.cloned.1.call-update) | async-done | bytes 4194320 | tf_op jit(solution)/shard_map/all_gather | solution.py:189
  289.2 16.6 %fusion.89 = f32[1024,2,2304]{2,0,1:T(8,128)} fusion(bf16[1024,2,1024]{2,0,1:T(8,128)(2,1)} %all-gather.9.cloned.1.call-done, bf16[1024,2304,1]{1,0,2:T(8,128)(2,1)} %reshape.287), kind=kOutput, calls=%fused_computation.189 | convolution fusion | flops 9663676416 | bytes 27787264 | tf_op jit(solution)/shard_map/lsd,de->lse/dot_general | solution.py:190
  305.9 39.2 %all-gather.13.cloned.1.call-done = bf16[1152,1024]{1,0:T(8,128)(2,1)} async-done(((bf16[1152,128]{1,0:T(8,128)(2,1)}), bf16[1152,1024]{1,0:T(8,128)(2,1)}) %all-gather.13.cloned.1.call-update) | async-done | bytes 2359312 | tf_op jit(solution)/shard_map/all_gather | solution.py:147
  345.0 34.2 %all-gather.15.cloned.1.call-done = bf16[1024,2,1024]{2,0,1:T(8,128)(2,1)} async-done(((bf16[256,2,1024]{2,0,1:T(8,128)(2,1)}), bf16[1024,2,1024]{2,0,1:T(8,128)(2,1)}) %all-gather.15.cloned.1.call-update) | async-done | bytes 4194320 | tf_op jit(solution)/shard_map/all_gather | solution.py:209
  379.2 16.5 %multiply_convert_fusion.1 = (bf16[1024,2,1152]{2,0,1:T(8,128)(2,1)}, bf16[1024,2,1152]{2,0,1:T(8,128)(2,1)}, bf16[1024,2,1152]{2,0,1:T(8,128)(2,1)}) fusion(f32[1024,2,2304]{2,0,1:T(8,128)} %fusion.89, bf16[1024,2,1024]{2,0,1:T(8,128)(2,1)} %all-gather.15.cloned.1.call-done, bf16[1152,1024]{1,0:T(8,128)(2,1)} %all-gather.13.cloned.1.call-done), kind=kOutput, calls=%fused_computation.77 | convolution fusion | flops 4869586944 | bytes 39583744 | tf_op jit(solution)/shard_map/xnw,jw->xnj/dot_general | solution.py:210
  395.7 15.9 %fusion.49 = f32[1024,2,1024]{2,0,1:T(8,128)} fusion(bf16[1024,2304,1]{1,0,2:T(8,128)(2,1)} %reshape.287, bf16[1024,2,1152]{2,0,1:T(8,128)(2,1)} %get-tuple-element.469, bf16[1024,2,1152]{2,0,1:T(8,128)(2,1)} %get-tuple-element.468), kind=kOutput, calls=%fused_computation.86 | convolution fusion | flops 9682550784 | bytes 22544384 | tf_op jit(solution)/shard_map/lse,de->lsd/dot_general | solution.py:225
  411.9 71.6 %reduce-scatter.12.cloned.1.call-done = f32[256,2,1024]{2,0,1:T(8,128)} async-done(((f32[1024,2,1024]{2,0,1:T(8,128)}), f32[256,2,1024]{2,0,1:T(8,128)}) %reduce-scatter.12.cloned.1.call-update) | async-done | bytes 2097168 | tf_op jit(solution)/shard_map/reduce_scatter | solution.py:224
  489.7 33.1 %all-gather.17.cloned.1.call-done = bf16[1024,2,1024]{2,0,1:T(8,128)(2,1)} async-done(((bf16[256,2,1024]{2,0,1:T(8,128)(2,1)}), bf16[1024,2,1024]{2,0,1:T(8,128)(2,1)}) %all-gather.17.cloned.1.call-update) | async-done | bytes 4194320 | tf_op jit(solution)/shard_map/all_gather | solution.py:233
  522.8 3.6 convolution_convert_fusion.2
  526.4 81.7 %while.59 = (s32[]{:T(128)}, f32[2,1024,2,2,64]{4,3,2,1,0:T(2,128)}, f32[2,1024,2,64]{1,3,2,0:T(8,128)}, bf16[2,1024,2,64]{1,3,2,0:T(8,128)(2,1)}, f32[2,2,2,2,5...) while((s32[]{:T(128)}, ...), condition=%wide.region_18.19_spmd, body=%wide.region_14.18_spmd.sunk | while | flops 1364983296 | bytes 96287368 | solution.py:248
  530.2 30.9 %while.61 = (s32[]{:T(128)}, f32[1024,2,64]{0,2,1:T(8,128)S(1)}, f32[1024,2,64]{0,2,1:T(8,128)S(1)}, f32[2,512,2,2,64]{1,4,3,2,0:T(8,128)}, s32[2]{0:T(128)S(1)}...) while((s32[]{:T(128)}, f32[1024,2,64]{0,2,1:T(8,128)S(1)}, ...), condition=%wide.region_17.17_spmd.clone.clone, body=%wide.region_15.16_spmd.clone.clone.sunk | while | flops 1364983296 | bytes 77379872 | solution.py:110
  535.9 4.3 fusion.135
  551.3 4.3 fusion.135
  561.2 2.9 copy.128
  571.0 30.9 %while.61 = (s32[]{:T(128)}, f32[1024,2,64]{0,2,1:T(8,128)S(1)}, f32[1024,2,64]{0,2,1:T(8,128)S(1)}, f32[2,512,2,2,64]{1,4,3,2,0:T(8,128)}, s32[2]{0:T(128)S(1)}...) while((s32[]{:T(128)}, f32[1024,2,64]{0,2,1:T(8,128)S(1)}, ...), condition=%wide.region_17.17_spmd.clone.clone, body=%wide.region_15.16_spmd.clone.clone.sunk | while | flops 1364983296 | bytes 77379872 | solution.py:110
  576.7 4.3 fusion.135
  592.1 4.3 fusion.135
  611.3 5.7 fusion.87
  616.9 3.5 copy.109
  620.4 3.5 copy.108
  633.1 5.6 convolution_convert_fusion
  638.7 9.6 convolution_convert_fusion.1
  648.4 17.2 %convolution_bitcast_fusion.1 = f32[1024,2304]{1,0:T(8,128)} fusion(bf16[1024,2,1024]{2,0,1:T(8,128)(2,1)} %all-gather.9.cloned.1.call-done, bf16[1024,2,1152]{2,0,1:T(8,128)(2,1)} %get-tuple-element.469, bf16[1024,2,1152]{2,0,1:T(8,128)(2,1)} %get-tuple-element.468), kind=kOutput, calls=%fused_computation.80 | convolution fusion | flops 9682550784 | bytes 23068672 | tf_op jit(solution)/shard_map/lsd,lse->de/dot_general | solution.py:220
  665.6 12.0 reshape.278
  679.0 9.7 convolution_bitcast_fusion.2
  688.9 4.9 convolution_bitcast_fusion.4
  698.7 44.4 %reduce-scatter.14.cloned.1.call-done = bf16[256,2,1024]{2,0,1:T(8,128)(2,1)} async-done(((bf16[1024,2,1024]{2,0,1:T(8,128)(2,1)}), bf16[256,2,1024]{2,0,1:T(8,128)(2,1)}) %reduce-scatter.14.cloned.1.call-update) | async-done | bytes 1048592 | tf_op jit(solution)/shard_map/reduce_scatter | solution.py:276
  745.2 44.7 %reduce-scatter.10.cloned.1.call-done = bf16[256,2,1024]{2,0,1:T(8,128)(2,1)} async-done(((bf16[1024,2,1024]{2,0,1:T(8,128)(2,1)}), bf16[256,2,1024]{2,0,1:T(8,128)(2,1)}) %reduce-scatter.10.cloned.1.call-update) | async-done | bytes 1048592 | tf_op jit(solution)/shard_map/reduce_scatter | solution.py:199
  789.9 3.7 fusion.60
  793.7 2.9 copy.92
  798.7 44.9 %all-reduce.2 = (f32[1024]{0:T(1024)}, f32[64]{0:T(128)}, f32[64]{0:T(128)}, f32[1024]{0:T(1024)}) all-reduce(f32[1024]{0:T(1024)S(1)} %get-tuple-element.378, f32[64]{0:T(128)S(1)} %reduce_sum.151, f32[64]{0:T(128)S(1)} %reduce_sum.154, f32[1024]{0:T(1024)S(1)} %copy-done.39), channel_id=1, replica_groups=mesh['dp'=8,'tensor'=4] {'dp','tensor'}, use_global_device_ids=true, to_apply=%region_29.30 | all-reduce | flops 2176 | bytes 17408 | tf_op jit(solution)/shard_map/psum | solution.py:293
  843.5 279.2 %all-reduce.6.cloned.1.call-done = (f32[1024,2,128]{2,1,0:T(2,128)}, f32[1024,2,1152]{2,1,0:T(2,128)}) async-done(((f32[1024,2,128]{2,1,0:T(2,128)}, f32[1024,2,1152]{2,1,0:T(2,128)}), (f32[1024,2,128]{2,1,0:T(2,128)}, f32[1024,2,1152]{2,1,0:T(2,128)})) %all-reduce.6.cloned.1.call-update) | async-done | bytes 10485776
  1126.7 94.9 %reduce-scatter.20.cloned.1.call-done = f32[1152,128]{1,0:T(8,128)} async-done(((f32[1152,1024]{1,0:T(8,128)}), f32[1152,128]{1,0:T(8,128)}) %reduce-scatter.20.cloned.1.call-update) | async-done | bytes 589840 | tf_op jit(solution)/shard_map/reduce_scatter | solution.py:291
  1221.6 67.5 %reduce-scatter.18.cloned.1.call-done = f32[256,128]{1,0:T(8,128)} async-done(((f32[256,1024]{1,0:T(8,128)}), f32[256,128]{1,0:T(8,128)}) %reduce-scatter.18.cloned.1.call-update) | async-done | bytes 131088 | tf_op jit(solution)/shard_map/reduce_scatter | solution.py:289
  (326 shorter events, 142.1 us)
Async XLA Ops:
  8.0 4.4 copy-start.29
  8.0 4.5 copy-start.27
  8.0 65.2 %copy-start.28 = (bf16[256,128]{1,0:T(8,128)(2,1)S(1)}, bf16[256,128]{1,0:T(8,128)(2,1)}, u32[]{:S(2)}) copy-start(bf16[256,128]{1,0:T(8,128)(2,1)} %param.24) | copy-start | bytes 196612
  8.0 95.0 %all-gather.7.cloned.1.call-start = ((), (), s32[]{:S(2)}) async-start(), calls=%async_computation.7 | async-start | bytes 5242880 | tf_op jit(solution)/shard_map/all_gather | solution.py:151
  12.3 232.0 %reduce-scatter.8.cloned.1.call-start = ((), (), s32[]{:S(2)}) async-start(), calls=%async_computation.8 | async-start | bytes 10485760 | tf_op jit(solution)/shard_map/reduce_scatter | solution.py:182
  46.1 61.6 %copy-start.21 = (bf16[1024,2,128]{0,2,1:T(8,128)(2,1)}, bf16[1024,2,128]{0,2,1:T(8,128)(2,1)S(1)}, u32[]{:S(2)}) copy-start(bf16[1024,2,128]{0,2,1:T(8,128)(2,1)S(1)} %copy.80) | copy-start | bytes 1572868
  73.3 34.4 %copy-start.19 = (bf16[1024,256]{0,1:T(8,128)(2,1)}, bf16[1024,256]{0,1:T(8,128)(2,1)S(1)}, u32[]{:S(2)}) copy-start(bf16[1024,256]{0,1:T(8,128)(2,1)S(1)} %all_gather.28) | copy-start | bytes 1572868
  103.0 6.8 copy-start.15
  167.8 6.5 copy-start.4
  167.8 6.5 copy-start.10
  174.3 70.0 %copy-start.7 = (bf16[256,2,1024]{2,1,0:T(2,128)(2,1)S(1)}, bf16[256,2,1024]{2,1,0:T(2,128)(2,1)}, u32[]{:S(2)}) copy-start(bf16[256,2,1024]{2,1,0:T(2,128)(2,1)} %param.20) | copy-start | bytes 3145732
  174.3 72.1 %copy-start.30 = (f32[1024]{0:T(1024)S(1)}, f32[1024]{0:T(1024)}, u32[]{:S(2)}) copy-start(f32[1024]{0:T(1024)} %param.30) | copy-start | bytes 12292
  174.4 80.2 %all-gather.11.cloned.1.call-start = ((), (), s32[]{:S(2)}) async-start(), calls=%async_computation.10 | async-start | bytes 5308416 | tf_op jit(solution)/shard_map/all_gather | solution.py:146
  174.9 114.3 %all-gather.9.cloned.1.call-start = ((), (), s32[]{:S(2)}) async-start(), calls=%async_computation.9 | async-start | bytes 5242880 | tf_op jit(solution)/shard_map/all_gather | solution.py:189
  246.4 240.0 %copy-start = (f32[256,2,1024]{2,0,1:T(8,128)}, f32[256,2,1024]{2,0,1:T(8,128)S(1)}, u32[]{:S(2)}) copy-start(f32[256,2,1024]{2,0,1:T(8,128)S(1)} %get-tuple-element.459) | copy-start | bytes 6291460
  246.4 240.0 %copy-start.32 = (f32[256,2]{0,1:T(2,128)}, f32[256,2]{0,1:T(2,128)S(1)}, u32[]{:S(2)}) copy-start(f32[256,2]{0,1:T(2,128)S(1)} %add_rsqrt_fusion.2) | copy-start | bytes 6148
  247.9 97.1 %all-gather.13.cloned.1.call-start = ((), (), s32[]{:S(2)}) async-start(), calls=%async_computation.11 | async-start | bytes 2654208 | tf_op jit(solution)/shard_map/all_gather | solution.py:147
  248.5 130.7 %all-gather.15.cloned.1.call-start = ((), (), s32[]{:S(2)}) async-start(), calls=%async_computation.13 | async-start | bytes 5242880 | tf_op jit(solution)/shard_map/all_gather | solution.py:209
  248.6 237.8 %copy-start.40 = (pred[256,2]{0,1:T(4,128)(4,1)}, pred[256,2]{0,1:T(4,128)(4,1)S(1)}, u32[]{:S(2)}) copy-start(pred[256,2]{0,1:T(4,128)(4,1)S(1)} %broadcast_compare_fusion) | copy-start | bytes 1540
  251.1 232.4 %reduce-scatter.12.cloned.1.call-start = ((), (), s32[]{:S(2)}) async-start(), calls=%async_computation.14 | async-start | bytes 10485760 | tf_op jit(solution)/shard_map/reduce_scatter | solution.py:224
  411.7 74.8 %copy-start.12 = (bf16[256,2,1024]{2,1,0:T(2,128)(2,1)S(1)}, bf16[256,2,1024]{2,1,0:T(2,128)(2,1)}, u32[]{:S(2)}) copy-start(bf16[256,2,1024]{2,1,0:T(2,128)(2,1)} %param.31) | copy-start | bytes 3145732
  411.7 111.1 %all-gather.17.cloned.1.call-start = ((), (), s32[]{:S(2)}) async-start(), calls=%async_computation.15 | async-start | bytes 5242880 | tf_op jit(solution)/shard_map/all_gather | solution.py:233
  483.5 2.9 copy-start.9
  486.5 39.9 %copy-start.37 = (f32[256,2]{0,1:T(2,128)}, f32[256,2]{0,1:T(2,128)S(1)}, u32[]{:S(2)}) copy-start(f32[256,2]{0,1:T(2,128)S(1)} %broadcast_multiply_fusion.3) | copy-start | bytes 6148
  488.4 208.7 %reduce-scatter.16.cloned.1.call-start = ((), (), s32[]{:S(2)}) async-start(), calls=%async_computation.17 | async-start | bytes 1179648 | tf_op jit(solution)/shard_map/reduce_scatter | solution.py:287
  526.4 81.7 %copy-start.16 = (f32[1024,32]{0,1:T(8,128)S(1)}, f32[1024,32]{0,1:T(8,128)}, u32[]{:S(2)}) copy-start(f32[1024,32]{0,1:T(8,128)} %copy-done.15) | copy-start | bytes 393220
  526.4 81.7 %copy-start.17 = (f32[1024,32]{0,1:T(8,128)S(1)}, f32[1024,32]{0,1:T(8,128)}, u32[]{:S(2)}) copy-start(f32[1024,32]{0,1:T(8,128)} %get-tuple-element.493) | copy-start | bytes 393220
  526.4 83.2 %copy-start.48 = (f32[64]{0:T(128)S(1)}, f32[64]{0:T(128)}, u32[]{:S(2)}) copy-start(f32[64]{0:T(128)} %param.29) | copy-start | bytes 772
  526.4 2.7 copy-start.13
  567.1 2.8 copy-start.13
  608.1 3.2 copy-start.11
  620.4 3.8 copy-start.44
  627.3 4.4 copy-start.18
  632.9 110.2 %reduce-scatter.14.cloned.1.call-start = ((), (), s32[]{:S(2)}) async-start(), calls=%async_computation.16 | async-start | bytes 5242880 | tf_op jit(solution)/shard_map/reduce_scatter | solution.py:276
  638.7 151.2 %reduce-scatter.10.cloned.1.call-start = ((), (), s32[]{:S(2)}) async-start(), calls=%async_computation.12 | async-start | bytes 5242880 | tf_op jit(solution)/shard_map/reduce_scatter | solution.py:199
  648.3 474.4 %all-reduce.6.cloned.1.call-start = ((), (), s32[]{:S(2)}) async-start(), calls=%async_computation.20 | async-start | bytes 20971520
  678.9 542.7 %reduce-scatter.20.cloned.1.call-start = ((), (), s32[]{:S(2)}) async-start(), calls=%async_computation.19 | async-start | bytes 5308416 | tf_op jit(solution)/shard_map/reduce_scatter | solution.py:291
  688.7 5.1 copy-start.53
  688.7 54.3 %copy-start.8 = (bf16[256,2,1024]{2,1,0:T(2,128)(2,1)S(1)}, bf16[256,2,1024]{2,1,0:T(2,128)(2,1)}, u32[]{:S(2)}) copy-start(bf16[256,2,1024]{2,1,0:T(2,128)(2,1)} %param.20) | copy-start | bytes 3145732
  688.7 54.3 %copy-start.34 = (f32[1024]{0:T(1024)S(1)}, f32[1024]{0:T(1024)}, u32[]{:S(2)}) copy-start(f32[1024]{0:T(1024)} %param.27) | copy-start | bytes 12292
  688.8 54.3 %copy-start.36 = (f32[256,2]{0,1:T(2,128)S(1)}, f32[256,2]{0,1:T(2,128)}, u32[]{:S(2)}) copy-start(f32[256,2]{0,1:T(2,128)} %copy-done.35) | copy-start | bytes 6148
  688.8 101.1 %copy-start.1 = (f32[256,2,1024]{2,0,1:T(8,128)S(1)}, f32[256,2,1024]{2,0,1:T(8,128)}, u32[]{:S(2)}) copy-start(f32[256,2,1024]{2,0,1:T(8,128)} %copy-done) | copy-start | bytes 6291460
  688.8 101.1 %copy-start.31 = (f32[1024]{0:T(1024)S(1)}, f32[1024]{0:T(1024)}, u32[]{:S(2)}) copy-start(f32[1024]{0:T(1024)} %param.30) | copy-start | bytes 12292
  688.8 101.1 %copy-start.33 = (f32[256,2]{0,1:T(2,128)S(1)}, f32[256,2]{0,1:T(2,128)}, u32[]{:S(2)}) copy-start(f32[256,2]{0,1:T(2,128)} %copy-done.32) | copy-start | bytes 6148
  688.8 101.1 %copy-start.38 = (f32[256,2]{0,1:T(2,128)S(1)}, f32[256,2]{0,1:T(2,128)}, u32[]{:S(2)}) copy-start(f32[256,2]{0,1:T(2,128)} %copy-done.37) | copy-start | bytes 6148
  688.8 101.1 %copy-start.41 = (pred[256,2]{0,1:T(4,128)(4,1)S(1)}, pred[256,2]{0,1:T(4,128)(4,1)}, u32[]{:S(2)}) copy-start(pred[256,2]{0,1:T(4,128)(4,1)} %copy-done.40) | copy-start | bytes 1540
  688.8 600.3 %reduce-scatter.18.cloned.1.call-start = ((), (), s32[]{:S(2)}) async-start(), calls=%async_computation.18 | async-start | bytes 1179648 | tf_op jit(solution)/shard_map/reduce_scatter | solution.py:289
  793.7 5.0 copy-start.39
  (28 other events, 45.7 us)
Sparse Core Ops, SparseCore 0:
  12.4 37.1 all-gather.6
  174.5 69.7 reduce-scatter.7
  411.8 71.6 reduce-scatter.11
Sparse Core Ops, SparseCore 1:
  177.0 77.5 all-gather.10
  256.6 32.6 all-gather.8
  291.4 53.6 all-gather.12
  346.7 32.5 all-gather.14
  488.4 34.3 all-gather.16
  633.0 64.0 reduce-scatter.15
  699.6 43.4 reduce-scatter.13
  745.4 44.4 reduce-scatter.9
  794.4 328.3 all-reduce.5
  1127.0 94.5 reduce-scatter.19
  1225.5 63.6 reduce-scatter.17
where the time goes:
time: 1310 us; the launch traced here: 1300 us
  waiting for transfers between devices  808 us (62%)
  matrix products  170 us (13%)
  blocking collectives  134 us (10%)
  local copies, waits for them, and re-layouts  93.7 us (7%)
  other arithmetic  57.4 us (4%)
  between operations  17.2 us (1%)
  loops' own time  16.2 us (1%)
    unnamed x15, waiting for transfers between devices  280 us
    reduce_scatter x1, waiting for transfers between devices, local(): lax.psum_scatter(down_gradient, 'dp', scatter_dimension=1, tiled=True)  94.9 us
    reduce_scatter x1, waiting for transfers between devices, local(): lax.psum_scatter(jnp.einsum('lse,de->lsd', token_rows, inner_flat, prefer...  71.6 us
    reduce_scatter x1, waiting for transfers between devices, local(): lax.psum_scatter(jnp.einsum('lse,ed->lsd', token_rows, output_full, prefe...  69.3 us
    reduce_scatter x1, waiting for transfers between devices, local(): lax.psum_scatter(output_gradient, 'dp', scatter_dimension=1, tiled=True)  67.5 us
    psum x1, blocking collectives, local(): lax.psum((mixer_gain_part, query_gain_part, key_gain_part, dense_gain_par...  44.9 us
    reduce_scatter x1, waiting for transfers between devices, local(): lax.psum_scatter(jnp.einsum('pex,xa->pea', token_rows, complete_down_weig...  44.7 us
    reduce_scatter x1, waiting for transfers between devices, local(): lax.psum_scatter(jnp.einsum('lse,de->lsd', token_rows, joint_weight, pref...  44.4 us
  transfers between devices with their start and end apart: 14, of which 13 were waited for; matrix products, arithmetic and copies ran while one was open for 9% of the time, Pallas kernels for 0%

commit v1 on v0

v1 whole, which is shorter than its diff:
```python
import functools

import jax
import jax.numpy as jnp
from jax import lax
from jax.experimental import pallas as pl
from jax.experimental.pallas import tpu as pltpu
from jax.sharding import PartitionSpec as P

EPS = 1e-05
THETA = 1000000.0
LOG2E = 1.4426950408889634
F32 = jnp.float32
BF16 = jnp.bfloat16
HIGH = lax.Precision.HIGHEST
LANES = 128
VMEM_LIMIT = 56 * 1024 * 1024
ANY = pl.BlockSpec(memory_space=pl.ANY)
VMEM = pl.BlockSpec(memory_space=pltpu.VMEM)
SMEM = pl.BlockSpec(memory_space=pltpu.SMEM)


def dot(a, b, **kw):
    return lax.dot_general(
        a, b, (((1,), (0,)), ((), ())), preferred_element_type=F32, **kw
    )


def dot_nt(a, b, **kw):
    return lax.dot_general(
        a, b, (((1,), (1,)), ((), ())), preferred_element_type=F32, **kw
    )


def dot_tn(a, b, **kw):
    return lax.dot_general(
        a, b, (((0,), (0,)), ((), ())), preferred_element_type=F32, **kw
    )


def iota(shape, axis):
    return lax.broadcasted_iota(jnp.int32, shape, axis)


def low_half(shape):
    return iota(shape, 1) % LANES < LANES // 2


def head_blocks(scale):
    shape = (LANES, LANES)
    return jnp.where(iota(shape, 0) // 64 == iota(shape, 1) // 64, scale, 0.0).astype(F32)


def partner(values):
    first = iota(values.shape, 1) % 64 < 32
    return jnp.where(first, pltpu.roll(values, LANES - 32, 1), pltpu.roll(values, 32, 1))


def rows_of(index, size):
    return pl.ds(pl.multiple_of(index * size, size), size)


def load_all(sources, targets, sems, first):
    copies = []
    for number, (source, target) in enumerate(zip(sources, targets)):
        copy = pltpu.make_async_copy(source, target, sems.at[first + number])
        copy.start()
        copies.append(copy)
    return copies


def shard_targets(w_refs, ws, me):
    size = w_refs[0].shape[0]
    if len(w_refs) == 1:
        return [ws]
    return [ws.at[rows_of(me ^ slot, size)] for slot in range(len(w_refs))]


def store_slots(whole, out_refs, me):
    if len(out_refs) == 1:
        out_refs[0][...] = whole[...]
        return
    keep_ref, send_ref = out_refs
    size = keep_ref.shape[1]
    for slot in range(2 * keep_ref.shape[0]):
        (send_ref if slot % 2 else keep_ref)[slot // 2] = whole[rows_of(me ^ slot, size), :]


def attn_fwd_kernel(parts, n_w, scal, cos_ref, sin_ref, gq_ref, gk_ref, *refs):
    x_refs, refs = refs[:parts], refs[parts:]
    w_refs, refs = refs[:n_w], refs[n_w:]
    (raw_ref, q_ref, k_ref, v_ref, att_ref, lse_ref, keep_ref, send_ref, xs, ws, kp, vp, acc, sems) = refs
    size = x_refs[0].shape[0]
    me_t, me_d, length = scal[0], scal[1], scal[2]
    copies = load_all(w_refs, shard_targets(w_refs, ws, me_d), sems, 0)
    copies += load_all(x_refs, [xs.at[rows_of(me_t ^ j, size)] for j in range(parts)], sems, n_w)
    for copy in copies:
        copy.wait()
    mean_of = head_blocks(1.0 / 64)
    low = low_half((size, LANES))
    factor = LOG2E / 8.0

    def project(r, carry):
        rows = rows_of(r, size)
        projected = dot(xs[rows, :], ws[:, :512])
        raw_ref[rows, :] = projected[:, :384]
        cosines, sines = cos_ref[rows, :], sin_ref[rows, :]

        def turned(values, gain):
            mean = dot(values * values, mean_of, precision=HIGH)
            normed = values * lax.rsqrt(mean + EPS) * gain
            return normed * cosines + partner(normed) * sines

        for g in range(2):
            lanes = slice(LANES * g, LANES * (g + 1))
            q_ref[rows, lanes] = turned(projected[:, lanes], gq_ref[...]).astype(BF16)
        keys = turned(projected[:, 256:384], gk_ref[...])
        values = projected[:, 384:512]
        k_ref[rows, :] = keys.astype(BF16)
        v_ref[rows, :] = values.astype(BF16)
        live = r * size + iota((size, LANES), 0) < length
        ones = jnp.where(live, 1.0, 0.0)
        values = jnp.where(live, values, 0.0)
        keys_swap, values_swap = pltpu.roll(keys, 64, 1), pltpu.roll(values, 64, 1)
        for g in range(2):
            for e in range(2):
                here = low if e == 0 else jnp.logical_not(low)
                kp[2 * g + e, rows, :] = jnp.where(here, keys if g == e else keys_swap, 0.0).astype(BF16)
                vp[2 * g + e, rows, :LANES] = jnp.where(here, values if g == e else values_swap, 0.0).astype(BF16)
                vp[2 * g + e, rows, LANES:] = jnp.where(here, ones, 0.0).astype(BF16)
        return carry

    lax.fori_loop(0, parts, project, 0)
    causal = iota((size, size), 1) <= iota((size, size), 0)

    def attend(i, carry):
        rows = rows_of(i, size)
        queries = [q_ref[rows, LANES * g : LANES * (g + 1)] for g in range(2)]

        def block(kb, masked):
            cols = rows_of(kb, size)
            sums = []
            for g in range(2):
                total = None
                for e in range(2):
                    weights = jnp.exp2(dot_nt(queries[g], kp[2 * g + e, cols, :]) * factor)
                    if masked:
                        weights = jnp.where(causal, weights, 0.0)
                    part = dot(weights.astype(BF16), vp[2 * g + e, cols, :])
                    total = part if total is None else total + part
                sums.append(total)
            return sums

        for g, total in enumerate(block(i, True)):
            acc[g] = total

        def more(kb, carry):
            for g, total in enumerate(block(kb, False)):
                acc[g] += total
            return carry

        lax.fori_loop(0, i, more, 0)
        for g in range(2):
            lanes = slice(LANES * g, LANES * (g + 1))
            summed = acc[g, :, LANES:]
            att_ref[rows, lanes] = (acc[g, :, :LANES] / summed).astype(BF16)
            lse_ref[rows, lanes] = jnp.log2(summed)
        return carry

    lax.fori_loop(0, parts, attend, 0)
    for j in range(parts):
        out = dot_nt(att_ref[rows_of(me_t ^ j, size), :], ws[:, 512:])
        (send_ref if j % 2 else keep_ref)[j // 2] = out.astype(BF16)


def attn_fwd(scal, cosines, sines, gq, gk, x_parts, w_parts):
    parts, n_w = len(x_parts), len(w_parts)
    size, width = x_parts[0].shape
    full = parts * size
    cols = w_parts[0].shape[1]
    pair = jax.ShapeDtypeStruct((parts // 2, size, width), BF16)
    return pl.pallas_call(
        functools.partial(attn_fwd_kernel, parts, n_w),
        out_shape=(
            jax.ShapeDtypeStruct((full, 384), F32),
            jax.ShapeDtypeStruct((full, 256), BF16),
            jax.ShapeDtypeStruct((full, 128), BF16),
            jax.ShapeDtypeStruct((full, 128), BF16),
            jax.ShapeDtypeStruct((full, 256), BF16),
            jax.ShapeDtypeStruct((full, 256), F32),
            pair,
            pair,
        ),
        in_specs=[SMEM] + [VMEM] * 4 + [ANY] * (parts + n_w),
        out_specs=(VMEM,) * 8,
        scratch_shapes=[
            pltpu.VMEM((full, width), BF16),
            pltpu.VMEM((width, cols), BF16),
            pltpu.VMEM((4, full, LANES), BF16),
            pltpu.VMEM((4, full, 2 * LANES), BF16),
            pltpu.VMEM((2, size, 2 * LANES), F32),
            pltpu.SemaphoreType.DMA((n_w + parts,)),
        ],
        compiler_params=pltpu.CompilerParams(vmem_limit_bytes=VMEM_LIMIT),
        cost_estimate=pl.CostEstimate(flops=8_000_000_000, bytes_accessed=12_000_000, transcendentals=3_000_000),
        name="attention_forward",
    )(scal, cosines, sines, gq, gk, *x_parts, *w_parts)


def attn_bwd_kernel(parts, n_w, scal, cos_ref, sin_ref, gq_ref, gk_ref, raw_ref, q_ref, k_ref, v_ref, att_ref, lse_ref, *refs):
    x_refs, refs = refs[:parts], refs[parts:]
    r_refs, refs = refs[:parts], refs[parts:]
    w_refs, refs = refs[:n_w], refs[n_w:]
    n_g = 1 if n_w == 1 else 2
    keep_ref, send_ref, gains_ref = refs[:3]
    g_refs, refs = refs[3 : 3 + n_g], refs[3 + n_g :]
    xs, gs, ws, kp, vp, kt, ga, dq, dk, dv, gp, whole, lrow, drow, acc, sems = refs
    size = x_refs[0].shape[0]
    full = parts * size
    me_t, me_d, length = scal[0], scal[1], scal[2]
    copies = load_all(w_refs, shard_targets(w_refs, ws, me_d), sems, 0)
    copies += load_all(r_refs, [gs.at[rows_of(me_t ^ j, size)] for j in range(parts)], sems, n_w)
    copies += load_all(x_refs, [xs.at[rows_of(me_t ^ j, size)] for j in range(parts)], sems, n_w + parts)
    for copy in copies:
        copy.wait()
    mean_of = head_blocks(1.0 / 64)
    low = low_half((size, LANES))
    factor = LOG2E / 8.0
    pick = jnp.where(iota((8, 256), 0) == iota((8, 256), 1) // 64, 1.0, 0.0).astype(F32)

    def prepare(r, carry):
        rows = rows_of(r, size)
        grad = dot(gs[rows, :], ws[:, 512:]).astype(BF16)
        ga[rows, :] = grad
        drow[:, rows] = dot_nt(pick, grad.astype(F32) * att_ref[rows, :].astype(F32), precision=HIGH)
        lrow[:, rows] = dot_nt(pick * (1.0 / 64), lse_ref[rows, :], precision=HIGH)
        live = r * size + iota((size, LANES), 0) < length
        keys = jnp.where(live, k_ref[rows, :].astype(F32), 0.0)
        values = jnp.where(live, v_ref[rows, :].astype(F32), 0.0)
        keys_swap, values_swap = pltpu.roll(keys, 64, 1), pltpu.roll(values, 64, 1)
        for g in range(2):
            for e in range(2):
                here = low if e == 0 else jnp.logical_not(low)
                padded = jnp.where(here, keys if g == e else keys_swap, 0.0)
                kp[2 * g + e, rows, :] = padded.astype(BF16)
                kt[2 * g + e, :, rows] = padded.T.astype(BF16)
                vp[2 * g + e, rows, :] = jnp.where(here, values if g == e else values_swap, 0.0).astype(BF16)
        return carry

    lax.fori_loop(0, parts, prepare, 0)
    dk[...] = jnp.zeros_like(dk)
    dv[...] = jnp.zeros_like(dv)
    causal = iota((size, size), 0) <= iota((size, size), 1)
    low2 = iota((2 * size, LANES), 0) // size == iota((2 * size, LANES), 1) // 64

    def sweep(i, carry):
        rows = rows_of(i, size)
        queries, grads, queries2, grads2 = [], [], [], []
        for g in range(2):
            lanes = slice(LANES * g, LANES * (g + 1))
            queries.append(q_ref[rows, lanes])
            grads.append(ga[rows, lanes])
            for source, target in ((queries, queries2), (grads, grads2)):
                both = jnp.concatenate([source[g], source[g]], axis=0)
                target.append(jnp.where(low2, both, jnp.zeros_like(both)))

        def block(kb, masked):
            cols = rows_of(kb, size)
            parts_t = []
            for g in range(2):
                weights2, scores2, turned = [], [], None
                for e in range(2):
                    h = 2 * g + e
                    weights = jnp.exp2(dot_nt(kp[h, cols, :], queries[g]) * factor - lrow[h : h + 1, rows])
                    if masked:
                        weights = jnp.where(causal, weights, 0.0)
                    grad_weights = dot_nt(vp[h, cols, :], grads[g])
                    grad_scores = (weights * (grad_weights - drow[h : h + 1, rows])).astype(BF16)
                    weights2.append(weights.astype(BF16))
                    scores2.append(grad_scores)
                    part = dot(kt[h, :, cols], grad_scores)
                    turned = part if turned is None else turned + part
                dv[g, cols, :] += dot(jnp.concatenate(weights2, axis=1), grads2[g])
                dk[g, cols, :] += dot(jnp.concatenate(scores2, axis=1), queries2[g])
                parts_t.append(turned)
            return parts_t

        for g, total in enumerate(block(i, True)):
            acc[g] = total

        def more(kb, carry):
            for g, total in enumerate(block(kb, False)):
                acc[g] += total
            return carry

        lax.fori_loop(0, i, more, 0)
        for g in range(2):
            dq[rows, LANES * g : LANES * (g + 1)] = acc[g].T
        return carry

    lax.fori_loop(0, parts, sweep, 0)
    gains_ref[...] = jnp.zeros_like(gains_ref)

    def project(r, carry):
        rows = rows_of(r, size)
        cosines, sines = cos_ref[rows, :], sin_ref[rows, :]
        live = r * size + iota((size, LANES), 0) < length

        def back(grad, lanes, gain, row):
            raw = raw_ref[rows, lanes]
            rms = lax.rsqrt(dot(raw * raw, mean_of, precision=HIGH) + EPS)
            turned = grad * cosines - partner(grad) * sines
            gains_ref[row : row + 1, :] += jnp.sum(turned * raw * rms, axis=0, keepdims=True)
            weighted = turned * gain
            inner = dot(raw * weighted, mean_of, precision=HIGH)
            gp[rows, lanes] = (rms * weighted - raw * (rms * rms * rms) * inner).astype(BF16)

        def folded(ref):
            first, second = ref[0, rows, :], ref[1, rows, :]
            both = jnp.where(low, first + pltpu.roll(first, 64, 1), second + pltpu.roll(second, 64, 1))
            return jnp.where(live, both, 0.0)

        for g in range(2):
            lanes = slice(LANES * g, LANES * (g + 1))
            back(dq[rows, lanes] * 0.125, lanes, gq_ref[...], 0)
        back(folded(dk) * 0.125, slice(256, 384), gk_ref[...], 1)
        gp[rows, 384:512] = folded(dv).astype(BF16)
        return carry

    lax.fori_loop(0, parts, project, 0)
    for j in range(parts):
        out = dot_nt(gp[rows_of(me_t ^ j, size), :], ws[:, :512])
        (send_ref if j % 2 else keep_ref)[j // 2] = out.astype(BF16)

    def weigh(b, carry):
        rows = rows_of(b, 256)
        whole[rows, :512] = dot_tn(xs[:, rows], gp[...]).astype(BF16)
        whole[rows, 512:] = dot_tn(gs[:, rows], att_ref[...]).astype(BF16)
        return carry

    lax.fori_loop(0, whole.shape[0] // 256, weigh, 0)
    store_slots(whole, g_refs, me_d)


def slot_shapes(n_w, width, cols):
    if n_w == 1:
        return (jax.ShapeDtypeStruct((width, cols), BF16),)
    return (jax.ShapeDtypeStruct((n_w // 2, width // n_w, cols), BF16),) * 2


def attn_bwd(scal, cosines, sines, gq, gk, saved, x_parts, r_parts, w_parts):
    parts, n_w = len(x_parts), len(w_parts)
    size, width = x_parts[0].shape
    full = parts * size
    cols = w_parts[0].shape[1]
    pair = jax.ShapeDtypeStruct((parts // 2, size, width), BF16)
    g_shapes = slot_shapes(n_w, width, cols)
    outs = pl.pallas_call(
        functools.partial(attn_bwd_kernel, parts, n_w),
        out_shape=(pair, pair, jax.ShapeDtypeStruct((8, LANES), F32)) + g_shapes,
        in_specs=[SMEM] + [VMEM] * 10 + [ANY] * (2 * parts + n_w),
        out_specs=(VMEM,) * (3 + len(g_shapes)),
        scratch_shapes=[
            pltpu.VMEM((full, width), BF16),
            pltpu.VMEM((full, width), BF16),
            pltpu.VMEM((width, cols), BF16),
            pltpu.VMEM((4, full, LANES), BF16),
            pltpu.VMEM((4, full, LANES), BF16),
            pltpu.VMEM((4, LANES, full), BF16),
            pltpu.VMEM((full, 256), BF16),
            pltpu.VMEM((full, 256), F32),
            pltpu.VMEM((2, full, LANES), F32),
            pltpu.VMEM((2, full, LANES), F32),
            pltpu.VMEM((full, 512), BF16),
            pltpu.VMEM((width, cols), BF16),
            pltpu.VMEM((8, full), F32),
            pltpu.VMEM((8, full), F32),
            pltpu.VMEM((2, LANES, size), F32),
            pltpu.SemaphoreType.DMA((n_w + 2 * parts,)),
        ],
        compiler_params=pltpu.CompilerParams(vmem_limit_bytes=VMEM_LIMIT),
        cost_estimate=pl.CostEstimate(flops=14_000_000_000, bytes_accessed=15_000_000, transcendentals=3_000_000),
        name="attention_backward",
    )(scal, cosines, sines, gq, gk, *saved, *x_parts, *r_parts, *w_parts)
    return outs[0], outs[1], outs[2], outs[3:]


def ff_kernel(n_x, n_w, scal, *refs):
    x_refs, refs = refs[:n_x], refs[n_x:]
    u_refs, refs = refs[:n_x], refs[n_x:]
    w_refs, refs = refs[:n_w], refs[n_w:]
    n_g = 1 if n_w == 1 else 2
    hid_ref, ggu_ref = refs[:2]
    g_refs, refs = refs[2 : 2 + n_g], refs[2 + n_g :]
    xs, us, ws, whole, sems = refs
    size = x_refs[0].shape[0]
    me_d = scal[1]
    cols = ws.shape[1] // 3
    copies = load_all(w_refs, shard_targets(w_refs, ws, me_d), sems, 0)
    x_copies = load_all(x_refs, [xs.at[pl.ds(j * size, size)] for j in range(n_x)], sems, n_w)
    u_copies = load_all(u_refs, [us.at[pl.ds(j * size, size)] for j in range(n_x)], sems, n_w + n_x)
    for copy in copies + x_copies + u_copies:
        copy.wait()

    def tokens(r, carry):
        rows = rows_of(r, size)
        gate_up = dot(xs[rows, :], ws[:, : 2 * cols])
        grad = dot(us[rows, :], ws[:, 2 * cols :])
        gate, up = gate_up[:, :cols], gate_up[:, cols:]
        sig = 1.0 / (1.0 + jnp.exp2(gate * -LOG2E))
        silu = gate * sig
        hid_ref[rows, :] = (silu * up).astype(BF16)
        ggu_ref[rows, :cols] = (grad * up * (sig + silu * (1.0 - sig))).astype(BF16)
        ggu_ref[rows, cols:] = (grad * silu).astype(BF16)
        return carry

    lax.fori_loop(0, n_x, tokens, 0)

    def weigh(b, carry):
        rows = rows_of(b, 256)
        whole[rows, : 2 * cols] = dot_tn(xs[:, rows], ggu_ref[...]).astype(BF16)
        whole[rows, 2 * cols :] = dot_tn(us[:, rows], hid_ref[...]).astype(BF16)
        return carry

    lax.fori_loop(0, whole.shape[0] // 256, weigh, 0)
    store_slots(whole, g_refs, me_d)


def feed_forward(scal, x_parts, u_parts, w_parts):
    n_x, n_w = len(x_parts), len(w_parts)
    size, width = x_parts[0].shape
    full = n_x * size
    wide = w_parts[0].shape[1]
    cols = wide // 3
    g_shapes = slot_shapes(n_w, width, wide)
    outs = pl.pallas_call(
        functools.partial(ff_kernel, n_x, n_w),
        out_shape=(
            jax.ShapeDtypeStruct((full, cols), BF16),
            jax.ShapeDtypeStruct((full, 2 * cols), BF16),
        )
        + g_shapes,
        in_specs=[SMEM] + [ANY] * (2 * n_x + n_w),
        out_specs=(VMEM,) * (2 + len(g_shapes)),
        scratch_shapes=[
            pltpu.VMEM((full, width), BF16),
            pltpu.VMEM((full, width), BF16),
            pltpu.VMEM((width, wide), BF16),
            pltpu.VMEM((width, wide), BF16),
            pltpu.SemaphoreType.DMA((n_w + 2 * n_x,)),
        ],
        compiler_params=pltpu.CompilerParams(vmem_limit_bytes=VMEM_LIMIT),
        cost_estimate=pl.CostEstimate(flops=4 * full * width * wide, bytes_accessed=20_000_000, transcendentals=full * cols),
        name="feed_forward",
    )(scal, *x_parts, *u_parts, *w_parts)
    return outs[0], outs[1], outs[2:]


def ff_out_kernel(parts, n_c, n_w, seq, scal, *refs):
    hid_refs, refs = refs[:n_c], refs[n_c:]
    ggu_refs, refs = refs[:n_c], refs[n_c:]
    w_refs, refs = refs[: n_c * n_w], refs[n_c * n_w :]
    ykeep_ref, ysend_ref, gkeep_ref, gsend_ref, hs, gs, ws, sems = refs
    size = ykeep_ref.shape[1]
    full = parts * size
    me_d = scal[1]
    wide = ws.shape[2]
    cols = wide // 3
    copies = []
    first = 0
    for c in range(n_c):
        targets = shard_targets(w_refs[c * n_w : (c + 1) * n_w], ws.at[c], me_d)
        copies += load_all(w_refs[c * n_w : (c + 1) * n_w], targets, sems, first)
        first += n_w
    mine = pl.ds(seq * full, full)
    copies += load_all([ref.at[mine] for ref in ggu_refs], [gs.at[c] for c in range(n_c)], sems, first)
    copies += load_all([ref.at[mine] for ref in hid_refs], [hs.at[c] for c in range(n_c)], sems, first + n_c)
    for copy in copies:
        copy.wait()
    for j in range(parts):
        rows = pl.ds(j * size, size)
        grad = sum(dot_nt(gs[c, rows, :], ws[c, :, : 2 * cols]) for c in range(n_c))
        (gsend_ref if j % 2 else gkeep_ref)[j // 2] = grad.astype(BF16)
        out = sum(dot_nt(hs[c, rows, :], ws[c, :, 2 * cols :]) for c in range(n_c))
        (ysend_ref if j % 2 else ykeep_ref)[j // 2] = out.astype(BF16)


def ff_out(seq, scal, parts, size, hids, ggus, w_chunks):
    n_c, n_w = len(w_chunks), len(w_chunks[0])
    wide = w_chunks[0][0].shape[1]
    width = w_chunks[0][0].shape[0] * n_w
    full = parts * size
    cols = wide // 3
    pair = jax.ShapeDtypeStruct((parts // 2, size, width), BF16)
    return pl.pallas_call(
        functools.partial(ff_out_kernel, parts, n_c, n_w, seq),
        out_shape=(pair,) * 4,
        in_specs=[SMEM] + [ANY] * (2 * n_c + n_c * n_w),
        out_specs=(VMEM,) * 4,
        scratch_shapes=[
            pltpu.VMEM((n_c, full, cols), BF16),
            pltpu.VMEM((n_c, full, 2 * cols), BF16),
            pltpu.VMEM((n_c, width, wide), BF16),
            pltpu.SemaphoreType.DMA((n_c * n_w + 2 * n_c,)),
        ],
        compiler_params=pltpu.CompilerParams(vmem_limit_bytes=VMEM_LIMIT),
        cost_estimate=pl.CostEstimate(flops=2 * full * width * wide * n_c, bytes_accessed=22_000_000, transcendentals=0),
        name="feed_forward_out",
    )(scal, *hids, *ggus, *[shard for chunk in w_chunks for shard in chunk])


def swap(values, axis, bits):
    return lax.ppermute(values, axis, [(i, i ^ bits) for i in range(lax.axis_size(axis))])


def gather_tokens(block):
    far = swap(block, "tensor", 2)
    return [block, swap(block, "tensor", 1), far, swap(far, "tensor", 1)]


def scatter_tokens(keep, send):
    near = swap(send, "tensor", 1)
    middle = (keep[1].astype(F32) + near[1].astype(F32)).astype(BF16)
    far = swap(middle, "tensor", 2)
    return keep[0].astype(F32) + near[0].astype(F32) + far.astype(F32)


def gather_shards(shard):
    if lax.axis_size("dp") != 8 or shard.shape[0] % LANES:
        return [lax.all_gather(shard, "dp", axis=0, tiled=True)]
    slots = [shard, swap(shard, "dp", 1)]
    for bits in (2, 4, 6):
        there = swap(shard, "dp", bits)
        slots += [there, swap(there, "dp", 1)]
    return slots


def scatter_shards(grads):
    if len(grads) == 1:
        return lax.psum_scatter(grads[0].astype(F32), "dp", scatter_dimension=0, tiled=True)
    keep, send = grads
    near = swap(send, "dp", 1)
    both = keep.astype(F32) + near.astype(F32)
    total = both[0]
    for slot in (1, 2, 3):
        total = total + swap(both[slot].astype(BF16), "dp", 2 * slot).astype(F32)
    return total


def sum_everywhere(values):
    for axis in ("tensor", "dp"):
        bits = 1
        while bits < lax.axis_size(axis):
            values = values + swap(values, axis, bits)
            bits *= 2
    return values


def norm_rows(values, gain):
    factor = lax.rsqrt(jnp.mean(values * values, axis=-1, keepdims=True) + EPS)
    return (values * factor * gain, factor)


def norm_back(values, factor, gain, upstream):
    weighted = upstream * gain
    inner = jnp.mean(values * weighted, axis=-1, keepdims=True)
    return factor * weighted - values * factor * factor * factor * inner


def tables(full, head_width):
    half = head_width // 2
    freqs = THETA ** (-jnp.arange(half, dtype=F32) * 2.0 / head_width)
    angles = jnp.arange(full, dtype=F32)[:, None] * freqs[None, :]
    cosines, sines = jnp.cos(angles), jnp.sin(angles)
    return (jnp.tile(cosines, (1, 4)), jnp.tile(jnp.concatenate([-sines, sines], axis=1), (1, 2)))


def local(
    inputs,
    lengths,
    query_weight,
    key_value_weight,
    output_weight,
    inner_weight,
    down_weight,
    mixer_gain,
    query_gain,
    key_gain,
    dense_gain,
    cotangent,
):
    size, seqs, width = inputs.shape
    parts = lax.axis_size("tensor")
    full = size * parts
    head = query_gain.shape[0]
    query_cols = query_weight.shape[1]
    pair_cols = key_value_weight.shape[2]
    hidden = inner_weight.shape[2]
    shard = query_weight.shape[0]
    me_t, me_d = lax.axis_index("tensor"), lax.axis_index("dp")
    n_c = 3
    cols = hidden // n_c
    cosines, sines = tables(full, head)
    gq = jnp.tile(query_gain, 2)[None, :]
    gk = jnp.tile(key_gain, 2)[None, :]

    down_turned = down_weight.T
    attn_shard = jnp.concatenate(
        [query_weight, key_value_weight.reshape(shard, 2 * pair_cols), output_weight.T], axis=1
    )
    attn_w = gather_shards(attn_shard)
    positions = me_t * size + jnp.arange(size, dtype=jnp.int32)
    scals = [
        jnp.stack([me_t.astype(jnp.int32), me_d.astype(jnp.int32), lengths[s], jnp.int32(0)])
        for s in range(seqs)
    ]
    tokens = [inputs[:, s].astype(F32) for s in range(seqs)]
    valid = [(positions < lengths[s])[:, None] for s in range(seqs)]
    firsts = [norm_rows(tokens[s], mixer_gain) for s in range(seqs)]
    normed = [gather_tokens(firsts[s][0].astype(BF16)) for s in range(seqs)]
    ff_w = []
    for c in range(n_c):
        part = slice(c * cols, (c + 1) * cols)
        ff_w.append(
            gather_shards(
                jnp.concatenate(
                    [inner_weight[:, 0, part], inner_weight[:, 1, part], down_turned[:, part]], axis=1
                )
            )
        )
    upstream = [jnp.where(valid[s], cotangent[:, s].astype(F32), 0.0) for s in range(seqs)]
    up_parts = [gather_tokens(upstream[s].astype(BF16)) for s in range(seqs)]

    saved, residual, seconds, dense = [], [], [], []
    for s in range(seqs):
        outs = attn_fwd(scals[s], cosines, sines, gq, gk, normed[s], attn_w)
        saved.append(outs[:6])
        residual.append(tokens[s] + scatter_tokens(outs[6], outs[7]))
        dense_in, factor = norm_rows(residual[s], dense_gain)
        seconds.append(factor)
        dense.append(gather_tokens(dense_in.astype(BF16)))

    x_parts = [part for s in range(seqs) for part in dense[s]]
    u_parts = [part for s in range(seqs) for part in up_parts[s]]
    hids, ggus, ff_grads = [], [], []
    for c in range(n_c):
        hid, ggu, grads = feed_forward(scals[0], x_parts, u_parts, ff_w[c])
        hids.append(hid)
        ggus.append(ggu)
        ff_grads.append(scatter_shards(grads))

    block_out, input_gradient, attn_grads = [], [], []
    mixer_part = dense_part = gain_part = 0.0
    for s in range(seqs):
        ykeep, ysend, gkeep, gsend = ff_out(s, scals[s], parts, size, hids, ggus, ff_w)
        grad_dense = scatter_tokens(gkeep, gsend)
        dense_part = dense_part + jnp.sum(grad_dense * residual[s] * seconds[s], axis=0)
        grad_residual = upstream[s] + norm_back(residual[s], seconds[s], dense_gain, grad_dense)
        r_parts = gather_tokens(grad_residual.astype(BF16))
        nkeep, nsend, gains, grads = attn_bwd(
            scals[s], cosines, sines, gq, gk, saved[s], normed[s], r_parts, attn_w
        )
        attn_grads.append(grads)
        gain_part = gain_part + gains
        grad_normed = scatter_tokens(nkeep, nsend)
        factor = firsts[s][1]
        mixer_part = mixer_part + jnp.sum(grad_normed * tokens[s] * factor, axis=0)
        input_gradient.append(grad_residual + norm_back(tokens[s], factor, mixer_gain, grad_normed))
        out_sum = scatter_tokens(ykeep, ysend)
        block_out.append(jnp.where(valid[s], residual[s] + out_sum, 0.0).astype(BF16))

    summed = [
        sum(part.astype(F32) for part in parts_of).astype(BF16) for parts_of in zip(*attn_grads)
    ]
    attn_grad = scatter_shards(summed)
    early = sum_everywhere(jnp.concatenate([dense_part.reshape(-1, LANES), gain_part], axis=0))
    mixer = sum_everywhere(mixer_part.reshape(-1, LANES)).reshape(-1)
    dense_rows = width // LANES
    folded = early[dense_rows:, :head] + early[dense_rows:, head:]
    inner_gradient = jnp.stack(
        [
            jnp.concatenate([grad[:, p * cols : (p + 1) * cols] for grad in ff_grads], axis=1)
            for p in range(2)
        ],
        axis=1,
    )
    down_gradient = jnp.concatenate([grad[:, 2 * cols :] for grad in ff_grads], axis=1).T
    return (
        jnp.stack(block_out, axis=1),
        jnp.stack(input_gradient, axis=1),
        attn_grad[:, :query_cols],
        attn_grad[:, query_cols : query_cols + 2 * pair_cols].reshape(shard, 2, pair_cols),
        attn_grad[:, query_cols + 2 * pair_cols :].T,
        inner_gradient,
        down_gradient,
        mixer,
        folded[0],
        folded[1],
        early[:dense_rows].reshape(-1),
    )


def solution(mesh):
    return jax.shard_map(
        local,
        mesh=mesh,
        in_specs=(
            P("tensor", "dp", None),
            P("dp"),
            P("dp", "tensor"),
            P("dp", None, "tensor"),
            P("tensor", "dp"),
            P("dp", None, "tensor"),
            P("tensor", "dp"),
            P(),
            P(),
            P(),
            P(),
            P("tensor", "dp", None),
        ),
        out_specs=(
            P("tensor", "dp", None),
            P("tensor", "dp", None),
            P("dp", "tensor"),
            P("dp", None, "tensor"),
            P("tensor", "dp"),
            P("dp", None, "tensor"),
            P("tensor", "dp"),
            P(),
            P(),
            P(),
            P(),
        ),
        check_vma=False,
    )
```

time: 1310 us -> 610 us (0.47)
  waiting for transfers between devices: 808 us -> 241 us
  Pallas kernels: 0 us -> 184 us
  matrix products: 170 us -> 0 us
  blocking collectives: 134 us -> 0 us
  starting transfers between devices: 1.24 us -> 98.1 us
  local copies, waits for them, and re-layouts: 93.7 us -> 39.8 us
  other arithmetic: 57.4 us -> 36 us
  loops' own time: 16.2 us -> 0 us
  between operations: 17.2 us -> 2.38 us
    reduce_scatter x7 -> x0, waiting for transfers between devices: 394 us -> none  [the longest x1 94.9 us: local(): lax.psum_scatter(down_gradient, 'dp', scatter_dimension=1, tiled=True)]
    unnamed x15 -> x0, waiting for transfers between devices: 280 us -> none
    ppermute x0 -> x94, waiting for transfers between devices: none -> 241 us  [swap(): lax.ppermute(values, axis, [(i, i ^ bits) for i in range(lax.axis_size(ax...]
    pallas_call x0 -> x9, Pallas kernels: none -> 184 us  [the longest x3 60.5 us: feed_forward(): pl.pallas_call(functools.partial(ff_kernel, n_x, n_w), out_shape=(jax.Sha...]
    dot_general x40 -> x0, matrix products: 170 us -> none  [the longest x8 25 us: step(): jnp.einsum('qhgd,khd->hgqk', token_rows, keys, preferred_element_type=jnp...]
    all_gather x6 -> x0, waiting for transfers between devices: 133 us -> none  [the longest x1 39.2 us: local(): lax.all_gather(down_weight, 'dp', axis=1, tiled=True)]
    ppermute x0 -> x94, starting transfers between devices: none -> 98.1 us  [swap(): lax.ppermute(values, axis, [(i, i ^ bits) for i in range(lax.axis_size(ax...]
    all_gather x3 -> x0, blocking collectives: 88.9 us -> none  [the longest x1 33.1 us: local(): lax.all_gather(key_value_weight, 'dp', axis=0, tiled=True)]
  transfers between devices with their start and end apart: 14 -> 94, of which waited for: 13 -> 30; matrix products, arithmetic and copies ran while one was open for 9% -> 10% of each run, Pallas kernels for 0% -> 20%
where the time goes in v1:
time: 610 us; the launch traced here: 601 us
  waiting for transfers between devices  241 us (40%)
  Pallas kernels  184 us (30%)
  starting transfers between devices  98.1 us (16%)
  local copies, waits for them, and re-layouts  39.8 us (7%)
  other arithmetic  36 us (6%)
    ppermute x94, waiting for transfers between devices, swap(): lax.ppermute(values, axis, [(i, i ^ bits) for i in range(lax.axis_size(ax...  241 us
    ppermute x94, starting transfers between devices, swap(): lax.ppermute(values, axis, [(i, i ^ bits) for i in range(lax.axis_size(ax...  98.1 us
    pallas_call x3, Pallas kernels, feed_forward(): pl.pallas_call(functools.partial(ff_kernel, n_x, n_w), out_shape=(jax.Sha...  60.5 us
    pallas_call x2, Pallas kernels, attn_bwd(): pl.pallas_call(functools.partial(attn_bwd_kernel, parts, n_w), out_shape=...  59 us
    pallas_call x2, Pallas kernels, attn_fwd(): pl.pallas_call(functools.partial(attn_fwd_kernel, parts, n_w), out_shape=...  33.5 us
    pallas_call x2, Pallas kernels, ff_out(): pl.pallas_call(functools.partial(ff_out_kernel, parts, n_c, n_w, seq), ou...  31.5 us
    unnamed x170, local copies, waits for them, and re-layouts  17.9 us
  transfers between devices with their start and end apart: 94, of which 30 were waited for; matrix products, arithmetic and copies ran while one was open for 10% of the time, Pallas kernels for 20%

profile of v1, /device:TPU:0, one launch (start us, length us, event | category | flops | bytes accessed | tf_op | source)
XLA Modules:
  0.0 601.5 jit_solution(16112526212391163397)
XLA Ops:
  4.0 5.0 collective-permute-start.8
  9.6 3.4 fusion.71
  40.9 5.9 collective-permute-done.3.refs_5_.refs_9_
  48.5 2.6 collective-permute-done.9.refs_11_.refs_15_
  55.2 3.7 collective-permute-start.34
  62.9 16.7 %attention_forward.3 = (f32[1024,384]{1,0:T(8,128)}, bf16[1024,256]{1,0:T(8,128)(2,1)}, bf16[1024,128]{1,0:T(8,128)(2,1)}, bf16[1024,128]{1,0:T(8,128)(2,1)}, bf...) custom-call(s32[4]{0:T(128)} %pad_add_fusion.scal, ...), custom_call_target="tpu_custom_call" | custom-call | flops 8000000000 | bytes 12000000 | tf_op jit(solution)/shard_map/attention_forward/pallas_call | solution.py:182
  81.2 16.7 %attention_forward.2 = (f32[1024,384]{1,0:T(8,128)}, bf16[1024,256]{1,0:T(8,128)(2,1)}, bf16[1024,128]{1,0:T(8,128)(2,1)}, bf16[1024,128]{1,0:T(8,128)(2,1)}, bf...) custom-call(s32[4]{0:T(128)} %pad_add_fusion.1.scal, ...), custom_call_target="tpu_custom_call" | custom-call | flops 8000000000 | bytes 12000000 | tf_op jit(solution)/shard_map/attention_forward/pallas_call | solution.py:182
  103.2 12.4 %collective-permute-done.19 = bf16[256,1024]{1,0:T(8,128)(2,1)S(1)} collective-permute-done((bf16[256,1024]{1,0:T(8,128)(2,1)S(1)}, bf16[256,1024]{1,0:T(8,128)(2,1)S(1)}, u32[]{:S(2)}, u32[]{:S(2)}) %collective-permute-start.19) | collective-permute-done | bytes 524320 | tf_op jit(solution)/shard_map/ppermute | solution.py:513
  120.4 5.6 collective-permute-done.11
  129.3 12.8 %collective-permute-done.39.refs_20_.refs_18_ = bf16[128,1152]{1,0:T(8,128)(2,1)} collective-permute-done((bf16[128,1152]{1,0:T(8,128)(2,1)S(1)}, bf16[128,1152]{1,0:T(8,128)(2,1)}, u32[]{:S(2)}, u32[]{:S(2)}) %collective-permute-start.39) | collective-permute-done | bytes 294944 | tf_op jit(solution)/shard_map/ppermute | solution.py:513
  145.2 10.4 %collective-permute-done.46.refs_20_.refs_26_ = bf16[128,1152]{1,0:T(8,128)(2,1)S(1)} collective-permute-done((bf16[128,1152]{1,0:T(8,128)(2,1)S(1)}, bf16[128,1152]{1,0:T(8,128)(2,1)S(1)}, u32[]{:S(2)}, u32[]{:S(2)}) %collective-permute-start.46) | collective-permute-done | bytes 294944 | tf_op jit(solution)/shard_map/ppermute | solution.py:513
  159.8 10.6 %collective-permute-done.27.refs_14_ = bf16[256,1024]{1,0:T(8,128)(2,1)S(1)} collective-permute-done((bf16[256,1024]{1,0:T(8,128)(2,1)S(1)}, bf16[256,1024]{1,0:T(8,128)(2,1)S(1)}, u32[]{:S(2)}, u32[]{:S(2)}) %collective-permute-start.27) | collective-permute-done | bytes 524320 | tf_op jit(solution)/shard_map/ppermute | solution.py:513
  174.1 6.5 %collective-permute-done.47.refs_21_.refs_27_ = bf16[128,1152]{1,0:T(8,128)(2,1)S(1)} collective-permute-done((bf16[128,1152]{1,0:T(8,128)(2,1)S(1)}, bf16[128,1152]{1,0:T(8,128)(2,1)S(1)}, u32[]{:S(2)}, u32[]{:S(2)}) %collective-permute-start.47) | collective-permute-done | bytes 294944 | tf_op jit(solution)/shard_map/ppermute | solution.py:513
  180.6 3.2 collective-permute-done.45.refs_19_.refs_25_
  184.3 6.9 %collective-permute-done.13.refs_2_ = bf16[256,1024]{1,0:T(8,128)(2,1)S(1)} collective-permute-done((bf16[256,1024]{1,0:T(8,128)(2,1)S(1)}, bf16[256,1024]{1,0:T(8,128)(2,1)S(1)}, u32[]{:S(2)}, u32[]{:S(2)}) %collective-permute-start.13) | collective-permute-done | bytes 524320 | tf_op jit(solution)/shard_map/ppermute | solution.py:513
  196.7 20.1 %feed_forward.5 = (bf16[2048,384]{1,0:T(8,128)(2,1)}, bf16[2048,768]{1,0:T(8,128)(2,1)}, bf16[4,128,1152]{2,1,0:T(8,128)(2,1)}, bf16[4,128,1152]{2,1,0:T(8,128)(2,1)}) custom-call(s32[4]{0:T(128)} %pad_add_fusion.1.scal, bf16[256,1024]{1,0:T(8,128)(2,1)} %copy-done.34, bf16[256,1024]{1,0:T(8,128)(2,1)} %copy-done.56, bf16[256,1024]{1,0:T(8,128)(2,1)} %copy-done.53, ...), custom_call_target="tpu_custom_call" | custom-call | flops 9663676416 | bytes 20000000 | tf_op jit(solution)/shard_map/feed_forward/pallas_call | solution.py:436
  220.9 20.1 %feed_forward.4 = (bf16[2048,384]{1,0:T(8,128)(2,1)}, bf16[2048,768]{1,0:T(8,128)(2,1)}, bf16[4,128,1152]{2,1,0:T(8,128)(2,1)}, bf16[4,128,1152]{2,1,0:T(8,128)(2,1)}) custom-call(s32[4]{0:T(128)} %pad_add_fusion.1.scal, bf16[256,1024]{1,0:T(8,128)(2,1)} %copy-done.34, bf16[256,1024]{1,0:T(8,128)(2,1)} %copy-done.56, bf16[256,1024]{1,0:T(8,128)(2,1)} %copy-done.53, ...), custom_call_target="tpu_custom_call" | custom-call | flops 9663676416 | bytes 20000000 | tf_op jit(solution)/shard_map/feed_forward/pallas_call | solution.py:436
  241.1 3.9 collective-permute-done.31.refs_19_.refs_9_
  245.7 20.3 %feed_forward.3 = (bf16[2048,384]{1,0:T(8,128)(2,1)}, bf16[2048,768]{1,0:T(8,128)(2,1)}, bf16[4,128,1152]{2,1,0:T(8,128)(2,1)}, bf16[4,128,1152]{2,1,0:T(8,128)(2,1)}) custom-call(s32[4]{0:T(128)} %pad_add_fusion.1.scal, bf16[256,1024]{1,0:T(8,128)(2,1)} %copy-done.34, bf16[256,1024]{1,0:T(8,128)(2,1)} %copy-done.56, bf16[256,1024]{1,0:T(8,128)(2,1)} %copy-done.53, ...), custom_call_target="tpu_custom_call" | custom-call | flops 9663676416 | bytes 20000000 | tf_op jit(solution)/shard_map/feed_forward/pallas_call | solution.py:436
  266.0 15.7 %feed_forward_out.3 = (bf16[2,256,1024]{2,1,0:T(8,128)(2,1)}, bf16[2,256,1024]{2,1,0:T(8,128)(2,1)}, bf16[2,256,1024]{2,1,0:T(8,128)(2,1)}, bf16[2,256,1024]{2,1,0:T(8,128)(2,1)}) custom-call(s32[4]{0:T(128)} %pad_add_fusion.scal, bf16[2048,384]{1,0:T(8,128)(2,1)} %get-tuple-element.61.refs_0_, bf16[2048,384]{1,0:T(8,128)(2,1)} %get-tuple-element.62.refs_1_, ...), custom_call_target="tpu_custom_call" | custom-call | flops 7247757312 | bytes 22000000 | tf_op jit(solution)/shard_map/feed_forward_out/pallas_call | solution.py:495
  282.2 15.8 %feed_forward_out.2 = (bf16[2,256,1024]{2,1,0:T(8,128)(2,1)}, bf16[2,256,1024]{2,1,0:T(8,128)(2,1)}, bf16[2,256,1024]{2,1,0:T(8,128)(2,1)}, bf16[2,256,1024]{2,1,0:T(8,128)(2,1)}) custom-call(s32[4]{0:T(128)} %pad_add_fusion.1.scal, bf16[2048,384]{1,0:T(8,128)(2,1)} %get-tuple-element.61.refs_0_, bf16[2048,384]{1,0:T(8,128)(2,1)} %get-tuple-element.62.refs_1_, ...), custom_call_target="tpu_custom_call" | custom-call | flops 7247757312 | bytes 22000000 | tf_op jit(solution)/shard_map/feed_forward_out/pallas_call | solution.py:495
  306.4 21.3 %collective-permute-done.80 = bf16[4,128,1152]{2,1,0:T(8,128)(2,1)S(1)} collective-permute-done((bf16[4,128,1152]{2,1,0:T(8,128)(2,1)}, bf16[4,128,1152]{2,1,0:T(8,128)(2,1)S(1)}, u32[]{:S(2)}, u32[]{:S(2)}) %collective-permute-start.80) | collective-permute-done | bytes 1179680 | tf_op jit(solution)/shard_map/ppermute | solution.py:513
  329.8 23.1 %collective-permute-done.76 = bf16[4,128,1152]{2,1,0:T(8,128)(2,1)S(1)} collective-permute-done((bf16[4,128,1152]{2,1,0:T(8,128)(2,1)}, bf16[4,128,1152]{2,1,0:T(8,128)(2,1)S(1)}, u32[]{:S(2)}, u32[]{:S(2)}) %collective-permute-start.76) | collective-permute-done | bytes 1179680 | tf_op jit(solution)/shard_map/ppermute | solution.py:513
  352.9 2.3 collective-permute-start.83
  355.6 21.9 %collective-permute-done.72 = bf16[4,128,1152]{2,1,0:T(8,128)(2,1)S(1)} collective-permute-done((bf16[4,128,1152]{2,1,0:T(8,128)(2,1)}, bf16[4,128,1152]{2,1,0:T(8,128)(2,1)S(1)}, u32[]{:S(2)}, u32[]{:S(2)}) %collective-permute-start.72) | collective-permute-done | bytes 1179680 | tf_op jit(solution)/shard_map/ppermute | solution.py:513
  377.5 2.4 collective-permute-start.82
  382.4 21.4 %collective-permute-done.82 = bf16[128,1152]{1,0:T(8,128)(2,1)S(1)} collective-permute-done((bf16[128,1152]{1,0:T(8,128)(2,1)S(1)}, bf16[128,1152]{1,0:T(8,128)(2,1)S(1)}, u32[]{:S(2)}, u32[]{:S(2)}) %collective-permute-start.82) | collective-permute-done | bytes 294944 | tf_op jit(solution)/shard_map/ppermute | solution.py:513
  406.0 12.3 %collective-permute-done.78 = bf16[128,1152]{1,0:T(8,128)(2,1)S(1)} collective-permute-done((bf16[128,1152]{1,0:T(8,128)(2,1)S(1)}, bf16[128,1152]{1,0:T(8,128)(2,1)S(1)}, u32[]{:S(2)}, u32[]{:S(2)}) %collective-permute-start.78) | collective-permute-done | bytes 294944 | tf_op jit(solution)/shard_map/ppermute | solution.py:513
  419.9 2.2 collective-permute-start.75
  422.7 6.6 %collective-permute-start.74 = (bf16[128,1152]{1,0:T(8,128)(2,1)S(1)}, bf16[128,1152]{1,0:T(8,128)(2,1)S(1)}, u32[]{:S(2)}, u32[]{:S(2)}) collective-permute-start(bf16[128,1152]{1,0:T(8,128)(2,1)S(1)} %get-tuple-element.155), channel_id=1, source_target_pairs={{0,16},{4,20},{8,24},{12,28},{16,0},{20,4},{24,8},{28,12},{1,17},{... | collective-permute-start | bytes 884744 | tf_op jit(solution)/shard_map/ppermute | solution.py:513
  429.3 2.6 fusion.66
  432.0 2.8 fusion.68
  436.3 14.4 %collective-permute-done.74 = bf16[128,1152]{1,0:T(8,128)(2,1)S(1)} collective-permute-done((bf16[128,1152]{1,0:T(8,128)(2,1)S(1)}, bf16[128,1152]{1,0:T(8,128)(2,1)S(1)}, u32[]{:S(2)}, u32[]{:S(2)}) %collective-permute-start.74) | collective-permute-done | bytes 294944 | tf_op jit(solution)/shard_map/ppermute | solution.py:513
  453.2 12.3 %collective-permute-done.57.refs_6_ = bf16[256,1024]{1,0:T(8,128)(2,1)S(1)} collective-permute-done((bf16[256,1024]{1,0:T(8,128)(2,1)}, bf16[256,1024]{1,0:T(8,128)(2,1)S(1)}, u32[]{:S(2)}, u32[]{:S(2)}) %collective-permute-start.57) | collective-permute-done | bytes 524320 | tf_op jit(solution)/shard_map/ppermute | solution.py:513
  466.5 29.6 %attention_backward.3 = (bf16[2,256,1024]{2,1,0:T(8,128)(2,1)}, bf16[2,256,1024]{2,1,0:T(8,128)(2,1)}, f32[8,128]{1,0:T(8,128)}, bf16[4,128,768]{2,1,0:T(8,128)(2,1)}, bf16[4,128,768]{2,1,0:T(8,128)(2,1)}) custom-call(s32[4]{0:T(128)} %pad_add_fusion.scal, f32[1024,128]{1,0:T(8,128)} %copy.42.cos_ref, f32[1024,128]{1,0:T(8,128)} %copy.43.sin_ref, ...), custom_call_target="tpu_custom_call" | custom-call | flops 14000000000 | bytes 15000000 | tf_op jit(solution)/shard_map/attention_backward/pallas_call | solution.py:358
  497.2 29.4 %attention_backward.2 = (bf16[2,256,1024]{2,1,0:T(8,128)(2,1)}, bf16[2,256,1024]{2,1,0:T(8,128)(2,1)}, f32[8,128]{1,0:T(8,128)}, bf16[4,128,768]{2,1,0:T(8,128)(2,1)}, bf16[4,128,768]{2,1,0:T(8,128)(2,1)}) custom-call(s32[4]{0:T(128)} %pad_add_fusion.1.scal, f32[1024,128]{1,0:T(8,128)} %copy.42.cos_ref, f32[1024,128]{1,0:T(8,128)} %copy.43.sin_ref, ...), custom_call_target="tpu_custom_call" | custom-call | flops 14000000000 | bytes 15000000 | tf_op jit(solution)/shard_map/attention_backward/pallas_call | solution.py:358
  540.8 2.7 collective-permute-start.93
  546.4 7.1 %collective-permute-done.68 = bf16[4,128,768]{2,1,0:T(8,128)(2,1)} collective-permute-done((bf16[4,128,768]{2,1,0:T(8,128)(2,1)}, bf16[4,128,768]{2,1,0:T(8,128)(2,1)}, u32[]{:S(2)}, u32[]{:S(2)}) %collective-permute-start.68) | collective-permute-done | bytes 786464 | tf_op jit(solution)/shard_map/ppermute | solution.py:513
  558.9 2.2 collective-permute-start.71
  562.9 3.3 collective-permute-done.69
  566.2 3.7 collective-permute-done.71
  569.9 7.1 %collective-permute-done.70 = bf16[128,768]{1,0:T(8,128)(2,1)S(1)} collective-permute-done((bf16[128,768]{1,0:T(8,128)(2,1)S(1)}, bf16[128,768]{1,0:T(8,128)(2,1)S(1)}, u32[]{:S(2)}, u32[]{:S(2)}) %collective-permute-start.70) | collective-permute-done | bytes 196640 | tf_op jit(solution)/shard_map/ppermute | solution.py:513
  577.0 2.5 collective-permute-done.67
  579.5 2.3 fusion.19
  588.5 2.9 collective-permute-done.86
  591.3 3.1 fusion.15
  594.9 2.3 collective-permute-start.88
  597.5 2.9 copy.61
  (415 shorter events, 134.3 us)
Async XLA Ops:
  4.0 25.1 %collective-permute-start.8 = (bf16[128,768]{1,0:T(8,128)(2,1)}, bf16[128,768]{1,0:T(8,128)(2,1)}, u32[]{:S(2)}, u32[]{:S(2)}) collective-permute-start(bf16[128,768]{1,0:T(8,128)(2,1)} %pad_maximum_fusion.7.refs_4_.refs_8_), channel_id=1, source_target_pairs={{0,24},{4,28},{8,16},{12,20},{16,8},{20,12},{24,0},{28,4},{1,25},{... | collective-permute-start | bytes 589832 | tf_op jit(solution)/shard_map/ppermute | solution.py:513
  9.0 29.8 %collective-permute-start.6 = (bf16[128,768]{1,0:T(8,128)(2,1)}, bf16[128,768]{1,0:T(8,128)(2,1)}, u32[]{:S(2)}, u32[]{:S(2)}) collective-permute-start(bf16[128,768]{1,0:T(8,128)(2,1)} %pad_maximum_fusion.7.refs_4_.refs_8_), channel_id=1, source_target_pairs={{0,16},{4,20},{8,24},{12,28},{16,0},{20,4},{24,8},{28,12},{1,17},{... | collective-permute-start | bytes 589832 | tf_op jit(solution)/shard_map/ppermute | solution.py:513
  9.0 31.5 %collective-permute-start.4 = (bf16[128,768]{1,0:T(8,128)(2,1)}, bf16[128,768]{1,0:T(8,128)(2,1)}, u32[]{:S(2)}, u32[]{:S(2)}) collective-permute-start(bf16[128,768]{1,0:T(8,128)(2,1)} %pad_maximum_fusion.7.refs_4_.refs_8_), channel_id=1, source_target_pairs={{0,8},{4,12},{8,0},{12,4},{16,24},{20,28},{24,16},{28,20},{1,9},{5... | collective-permute-start | bytes 589832 | tf_op jit(solution)/shard_map/ppermute | solution.py:513
  16.7 44.4 %collective-permute-start.15 = (bf16[256,1024]{1,0:T(8,128)(2,1)}, bf16[256,1024]{1,0:T(8,128)(2,1)}, u32[]{:S(2)}, u32[]{:S(2)}) collective-permute-start(bf16[256,1024]{1,0:T(8,128)(2,1)} %get-tuple-element.203.refs_0_), channel_id=1, source_target_pairs={{0,1},{1,0},{2,3},{3,2},{4,5},{5,4},{6,7},{7,6},{8,9},{9,8},{10,11... | collective-permute-start | bytes 1572872 | tf_op jit(solution)/shard_map/ppermute | solution.py:513
  29.0 32.1 %collective-permute-start.1 = (bf16[256,1024]{1,0:T(8,128)(2,1)}, bf16[256,1024]{1,0:T(8,128)(2,1)}, u32[]{:S(2)}, u32[]{:S(2)}) collective-permute-start(bf16[256,1024]{1,0:T(8,128)(2,1)} %get-tuple-element.202.refs_0_), channel_id=1, source_target_pairs={{0,2},{1,3},{2,0},{3,1},{4,6},{5,7},{6,4},{7,5},{8,10},{9,11},{10,... | collective-permute-start | bytes 1572872 | tf_op jit(solution)/shard_map/ppermute | solution.py:513
  29.3 33.4 %collective-permute-start.17 = (bf16[256,1024]{1,0:T(8,128)(2,1)}, bf16[256,1024]{1,0:T(8,128)(2,1)}, u32[]{:S(2)}, u32[]{:S(2)}) collective-permute-start(bf16[256,1024]{1,0:T(8,128)(2,1)} %collective-permute-done.16.refs_2_), channel_id=1, source_target_pairs={{0,1},{1,0},{2,3},{3,2},{4,5},{5,4},{6,7},{7,6},{8,9},{9,8},{10,11... | collective-permute-start | bytes 1572872 | tf_op jit(solution)/shard_map/ppermute | solution.py:513
  55.2 62.6 %collective-permute-start.34 = (bf16[128,1152]{1,0:T(8,128)(2,1)}, bf16[128,1152]{1,0:T(8,128)(2,1)}, u32[]{:S(2)}, u32[]{:S(2)}) collective-permute-start(bf16[128,1152]{1,0:T(8,128)(2,1)} %pad_maximum_fusion.3.refs_16_.refs_6_), channel_id=1, source_target_pairs={{0,24},{4,28},{8,16},{12,20},{16,8},{20,12},{24,0},{28,4},{1,25},{... | collective-permute-start | bytes 884744 | tf_op jit(solution)/shard_map/ppermute | solution.py:513
  59.0 59.9 %collective-permute-start.32 = (bf16[128,1152]{1,0:T(8,128)(2,1)}, bf16[128,1152]{1,0:T(8,128)(2,1)}, u32[]{:S(2)}, u32[]{:S(2)}) collective-permute-start(bf16[128,1152]{1,0:T(8,128)(2,1)} %pad_maximum_fusion.3.refs_16_.refs_6_), channel_id=1, source_target_pairs={{0,16},{4,20},{8,24},{12,28},{16,0},{20,4},{24,8},{28,12},{1,17},{... | collective-permute-start | bytes 884744 | tf_op jit(solution)/shard_map/ppermute | solution.py:513
  61.1 18.5 %collective-permute-start = (bf16[256,1024]{1,0:T(8,128)(2,1)}, bf16[256,1024]{1,0:T(8,128)(2,1)S(1)}, u32[]{:S(2)}, u32[]{:S(2)}) collective-permute-start(bf16[256,1024]{1,0:T(8,128)(2,1)} %get-tuple-element.202.refs_0_), channel_id=1, source_target_pairs={{0,1},{1,0},{2,3},{3,2},{4,5},{5,4},{6,7},{7,6},{8,9},{9,8},{10,11... | collective-permute-start | bytes 1572872 | tf_op jit(solution)/shard_map/ppermute | solution.py:513
  61.1 67.2 %collective-permute-start.41 = (bf16[128,1152]{1,0:T(8,128)(2,1)}, bf16[128,1152]{1,0:T(8,128)(2,1)}, u32[]{:S(2)}, u32[]{:S(2)}) collective-permute-start(bf16[128,1152]{1,0:T(8,128)(2,1)} %pad_maximum_fusion.4.refs_16_.refs_14_), channel_id=1, source_target_pairs={{0,24},{4,28},{8,16},{12,20},{16,8},{20,12},{24,0},{28,4},{1,25},{... | collective-permute-start | bytes 884744 | tf_op jit(solution)/shard_map/ppermute | solution.py:513
  79.6 19.9 %collective-permute-start.18 = (bf16[2,256,1024]{2,1,0:T(8,128)(2,1)}, bf16[2,256,1024]{2,1,0:T(8,128)(2,1)S(1)}, u32[]{:S(2)}, u32[]{:S(2)}) collective-permute-start(bf16[2,256,1024]{2,1,0:T(8,128)(2,1)} %get-tuple-element.60), channel_id=1, source_target_pairs={{0,1},{1,0},{2,3},{3,2},{4,5},{5,4},{6,7},{7,6},{8,9},{9,8},{10,11... | collective-permute-start | bytes 3145736 | tf_op jit(solution)/shard_map/ppermute | solution.py:513
  102.6 23.4 %collective-permute-start.11 = (bf16[256,1024]{1,0:T(8,128)(2,1)S(1)}, bf16[256,1024]{1,0:T(8,128)(2,1)S(1)}, u32[]{:S(2)}, u32[]{:S(2)}) collective-permute-start(bf16[256,1024]{1,0:T(8,128)(2,1)S(1)} %fusion.43), channel_id=1, source_target_pairs={{0,2},{1,3},{2,0},{3,1},{4,6},{5,7},{6,4},{7,5},{8,10},{9,11},{10,... | collective-permute-start | bytes 1572872 | tf_op jit(solution)/shard_map/ppermute | solution.py:513
  115.5 26.5 %collective-permute-start.39 = (bf16[128,1152]{1,0:T(8,128)(2,1)S(1)}, bf16[128,1152]{1,0:T(8,128)(2,1)}, u32[]{:S(2)}, u32[]{:S(2)}) collective-permute-start(bf16[128,1152]{1,0:T(8,128)(2,1)S(1)} %copy-done.38), channel_id=1, source_target_pairs={{0,16},{4,20},{8,24},{12,28},{16,0},{20,4},{24,8},{28,12},{1,17},{... | collective-permute-start | bytes 884744 | tf_op jit(solution)/shard_map/ppermute | solution.py:513
  117.9 25.7 %collective-permute-start.37 = (bf16[128,1152]{1,0:T(8,128)(2,1)S(1)}, bf16[128,1152]{1,0:T(8,128)(2,1)}, u32[]{:S(2)}, u32[]{:S(2)}) collective-permute-start(bf16[128,1152]{1,0:T(8,128)(2,1)S(1)} %copy-done.38), channel_id=1, source_target_pairs={{0,8},{4,12},{8,0},{12,4},{16,24},{20,28},{24,16},{28,20},{1,9},{5... | collective-permute-start | bytes 884744 | tf_op jit(solution)/shard_map/ppermute | solution.py:513
  118.9 26.2 %collective-permute-start.48 = (bf16[128,1152]{1,0:T(8,128)(2,1)S(1)}, bf16[128,1152]{1,0:T(8,128)(2,1)S(1)}, u32[]{:S(2)}, u32[]{:S(2)}) collective-permute-start(bf16[128,1152]{1,0:T(8,128)(2,1)S(1)} %pad_maximum_fusion.5.refs_16_.refs_22_), channel_id=1, source_target_pairs={{0,24},{4,28},{8,16},{12,20},{16,8},{20,12},{24,0},{28,4},{1,25},{... | collective-permute-start | bytes 884744 | tf_op jit(solution)/shard_map/ppermute | solution.py:513
  126.0 29.6 %collective-permute-start.46 = (bf16[128,1152]{1,0:T(8,128)(2,1)S(1)}, bf16[128,1152]{1,0:T(8,128)(2,1)S(1)}, u32[]{:S(2)}, u32[]{:S(2)}) collective-permute-start(bf16[128,1152]{1,0:T(8,128)(2,1)S(1)} %pad_maximum_fusion.5.refs_16_.refs_22_), channel_id=1, source_target_pairs={{0,16},{4,20},{8,24},{12,28},{16,0},{20,4},{24,8},{28,12},{1,17},{... | collective-permute-start | bytes 884744 | tf_op jit(solution)/shard_map/ppermute | solution.py:513
  128.3 28.8 %collective-permute-start.44 = (bf16[128,1152]{1,0:T(8,128)(2,1)S(1)}, bf16[128,1152]{1,0:T(8,128)(2,1)S(1)}, u32[]{:S(2)}, u32[]{:S(2)}) collective-permute-start(bf16[128,1152]{1,0:T(8,128)(2,1)S(1)} %pad_maximum_fusion.5.refs_16_.refs_22_), channel_id=1, source_target_pairs={{0,8},{4,12},{8,0},{12,4},{16,24},{20,28},{24,16},{28,20},{1,9},{5... | collective-permute-start | bytes 884744 | tf_op jit(solution)/shard_map/ppermute | solution.py:513
  159.1 24.7 %collective-permute-start.25 = (bf16[256,1024]{1,0:T(8,128)(2,1)S(1)}, bf16[256,1024]{1,0:T(8,128)(2,1)S(1)}, u32[]{:S(2)}, u32[]{:S(2)}) collective-permute-start(bf16[256,1024]{1,0:T(8,128)(2,1)S(1)} %collective-permute-done.24.refs_10_), channel_id=1, source_target_pairs={{0,1},{1,0},{2,3},{3,2},{4,5},{5,4},{6,7},{7,6},{8,9},{9,8},{10,11... | collective-permute-start | bytes 1572872 | tf_op jit(solution)/shard_map/ppermute | solution.py:513
  159.3 25.0 %collective-permute-start.21 = (bf16[256,1024]{1,0:T(8,128)(2,1)S(1)}, bf16[256,1024]{1,0:T(8,128)(2,1)S(1)}, u32[]{:S(2)}, u32[]{:S(2)}) collective-permute-start(bf16[256,1024]{1,0:T(8,128)(2,1)S(1)} %get-tuple-element.200.refs_4_), channel_id=1, source_target_pairs={{0,2},{1,3},{2,0},{3,1},{4,6},{5,7},{6,4},{7,5},{8,10},{9,11},{10,... | collective-permute-start | bytes 1572872 | tf_op jit(solution)/shard_map/ppermute | solution.py:513
  170.4 20.8 %collective-permute-start.13 = (bf16[256,1024]{1,0:T(8,128)(2,1)S(1)}, bf16[256,1024]{1,0:T(8,128)(2,1)S(1)}, u32[]{:S(2)}, u32[]{:S(2)}) collective-permute-start(bf16[256,1024]{1,0:T(8,128)(2,1)S(1)} %get-tuple-element.201.refs_0_), channel_id=1, source_target_pairs={{0,2},{1,3},{2,0},{3,1},{4,6},{5,7},{6,4},{7,5},{8,10},{9,11},{10,... | collective-permute-start | bytes 1572872 | tf_op jit(solution)/shard_map/ppermute | solution.py:513
  191.2 25.6 %collective-permute-start.30 = (bf16[128,1152]{1,0:T(8,128)(2,1)}, bf16[128,1152]{1,0:T(8,128)(2,1)}, u32[]{:S(2)}, u32[]{:S(2)}) collective-permute-start(bf16[128,1152]{1,0:T(8,128)(2,1)} %pad_maximum_fusion.3.refs_16_.refs_6_), channel_id=1, source_target_pairs={{0,8},{4,12},{8,0},{12,4},{16,24},{20,28},{24,16},{28,20},{1,9},{5... | collective-permute-start | bytes 884744 | tf_op jit(solution)/shard_map/ppermute | solution.py:513
  191.3 26.9 %collective-permute-start.36 = (bf16[128,1152]{1,0:T(8,128)(2,1)S(1)}, bf16[128,1152]{1,0:T(8,128)(2,1)}, u32[]{:S(2)}, u32[]{:S(2)}) collective-permute-start(bf16[128,1152]{1,0:T(8,128)(2,1)S(1)} %copy-done.38), channel_id=1, source_target_pairs={{0,4},{4,0},{8,12},{12,8},{16,20},{20,16},{24,28},{28,24},{1,5},{5... | collective-permute-start | bytes 884744 | tf_op jit(solution)/shard_map/ppermute | solution.py:513
  192.9 26.0 %collective-permute-start.42 = (bf16[128,1152]{1,0:T(8,128)(2,1)}, bf16[128,1152]{1,0:T(8,128)(2,1)}, u32[]{:S(2)}, u32[]{:S(2)}) collective-permute-start(bf16[128,1152]{1,0:T(8,128)(2,1)} %collective-permute-done.41.refs_22_.refs_20_), channel_id=1, source_target_pairs={{0,4},{4,0},{8,12},{12,8},{16,20},{20,16},{24,28},{28,24},{1,5},{5... | collective-permute-start | bytes 884744 | tf_op jit(solution)/shard_map/ppermute | solution.py:513
  193.5 26.7 %collective-permute-start.40 = (bf16[128,1152]{1,0:T(8,128)(2,1)}, bf16[128,1152]{1,0:T(8,128)(2,1)}, u32[]{:S(2)}, u32[]{:S(2)}) collective-permute-start(bf16[128,1152]{1,0:T(8,128)(2,1)} %collective-permute-done.39.refs_20_.refs_18_), channel_id=1, source_target_pairs={{0,4},{4,0},{8,12},{12,8},{16,20},{20,16},{24,28},{28,24},{1,5},{5... | collective-permute-start | bytes 884744 | tf_op jit(solution)/shard_map/ppermute | solution.py:513
  196.0 25.0 %collective-permute-start.38 = (bf16[128,1152]{1,0:T(8,128)(2,1)}, bf16[128,1152]{1,0:T(8,128)(2,1)}, u32[]{:S(2)}, u32[]{:S(2)}) collective-permute-start(bf16[128,1152]{1,0:T(8,128)(2,1)} %collective-permute-done.37.refs_18_.refs_16_), channel_id=1, source_target_pairs={{0,4},{4,0},{8,12},{12,8},{16,20},{20,16},{24,28},{28,24},{1,5},{5... | collective-permute-start | bytes 884744 | tf_op jit(solution)/shard_map/ppermute | solution.py:513
  216.8 24.3 %collective-permute-start.29 = (bf16[128,1152]{1,0:T(8,128)(2,1)}, bf16[128,1152]{1,0:T(8,128)(2,1)S(1)}, u32[]{:S(2)}, u32[]{:S(2)}) collective-permute-start(bf16[128,1152]{1,0:T(8,128)(2,1)} %pad_maximum_fusion.3.refs_16_.refs_6_), channel_id=1, source_target_pairs={{0,4},{4,0},{8,12},{12,8},{16,20},{20,16},{24,28},{28,24},{1,5},{5... | collective-permute-start | bytes 884744 | tf_op jit(solution)/shard_map/ppermute | solution.py:513
  218.2 22.9 %collective-permute-start.35 = (bf16[128,1152]{1,0:T(8,128)(2,1)}, bf16[128,1152]{1,0:T(8,128)(2,1)S(1)}, u32[]{:S(2)}, u32[]{:S(2)}) collective-permute-start(bf16[128,1152]{1,0:T(8,128)(2,1)} %collective-permute-done.34.refs_22_.refs_12_), channel_id=1, source_target_pairs={{0,4},{4,0},{8,12},{12,8},{16,20},{20,16},{24,28},{28,24},{1,5},{5... | collective-permute-start | bytes 884744 | tf_op jit(solution)/shard_map/ppermute | solution.py:513
  218.9 22.2 %collective-permute-start.33 = (bf16[128,1152]{1,0:T(8,128)(2,1)}, bf16[128,1152]{1,0:T(8,128)(2,1)S(1)}, u32[]{:S(2)}, u32[]{:S(2)}) collective-permute-start(bf16[128,1152]{1,0:T(8,128)(2,1)} %collective-permute-done.32.refs_20_.refs_10_), channel_id=1, source_target_pairs={{0,4},{4,0},{8,12},{12,8},{16,20},{20,16},{24,28},{28,24},{1,5},{5... | collective-permute-start | bytes 884744 | tf_op jit(solution)/shard_map/ppermute | solution.py:513
  220.2 24.7 %collective-permute-start.31 = (bf16[128,1152]{1,0:T(8,128)(2,1)}, bf16[128,1152]{1,0:T(8,128)(2,1)S(1)}, u32[]{:S(2)}, u32[]{:S(2)}) collective-permute-start(bf16[128,1152]{1,0:T(8,128)(2,1)} %collective-permute-done.30.refs_18_.refs_8_), channel_id=1, source_target_pairs={{0,4},{4,0},{8,12},{12,8},{16,20},{20,16},{24,28},{28,24},{1,5},{5... | collective-permute-start | bytes 884744 | tf_op jit(solution)/shard_map/ppermute | solution.py:513
  281.8 20.2 %collective-permute-start.61 = (bf16[2,256,1024]{2,1,0:T(8,128)(2,1)}, bf16[2,256,1024]{2,1,0:T(8,128)(2,1)S(1)}, u32[]{:S(2)}, u32[]{:S(2)}) collective-permute-start(bf16[2,256,1024]{2,1,0:T(8,128)(2,1)} %get-tuple-element.82), channel_id=1, source_target_pairs={{0,1},{1,0},{2,3},{3,2},{4,5},{5,4},{6,7},{7,6},{8,9},{9,8},{10,11... | collective-permute-start | bytes 3145736 | tf_op jit(solution)/shard_map/ppermute | solution.py:513
  298.6 29.0 %collective-permute-start.80 = (bf16[4,128,1152]{2,1,0:T(8,128)(2,1)}, bf16[4,128,1152]{2,1,0:T(8,128)(2,1)S(1)}, u32[]{:S(2)}, u32[]{:S(2)}) collective-permute-start(bf16[4,128,1152]{2,1,0:T(8,128)(2,1)} %get-tuple-element.100), channel_id=1, source_target_pairs={{0,4},{4,0},{8,12},{12,8},{16,20},{20,16},{24,28},{28,24},{1,5},{5... | collective-permute-start | bytes 3538952 | tf_op jit(solution)/shard_map/ppermute | solution.py:513
  300.1 52.8 %collective-permute-start.76 = (bf16[4,128,1152]{2,1,0:T(8,128)(2,1)}, bf16[4,128,1152]{2,1,0:T(8,128)(2,1)S(1)}, u32[]{:S(2)}, u32[]{:S(2)}) collective-permute-start(bf16[4,128,1152]{2,1,0:T(8,128)(2,1)} %get-tuple-element.98), channel_id=1, source_target_pairs={{0,4},{4,0},{8,12},{12,8},{16,20},{20,16},{24,28},{28,24},{1,5},{5... | collective-permute-start | bytes 3538952 | tf_op jit(solution)/shard_map/ppermute | solution.py:513
  302.0 75.5 %collective-permute-start.72 = (bf16[4,128,1152]{2,1,0:T(8,128)(2,1)}, bf16[4,128,1152]{2,1,0:T(8,128)(2,1)S(1)}, u32[]{:S(2)}, u32[]{:S(2)}) collective-permute-start(bf16[4,128,1152]{2,1,0:T(8,128)(2,1)} %get-tuple-element.96), channel_id=1, source_target_pairs={{0,4},{4,0},{8,12},{12,8},{16,20},{20,16},{24,28},{28,24},{1,5},{5... | collective-permute-start | bytes 3538952 | tf_op jit(solution)/shard_map/ppermute | solution.py:513
  303.8 128.2 %collective-permute-start.53 = (bf16[256,1024]{1,0:T(8,128)(2,1)S(1)}, bf16[256,1024]{1,0:T(8,128)(2,1)S(1)}, u32[]{:S(2)}, u32[]{:S(2)}) collective-permute-start(bf16[256,1024]{1,0:T(8,128)(2,1)S(1)} %fusion.46), channel_id=1, source_target_pairs={{0,2},{1,3},{2,0},{3,1},{4,6},{5,7},{6,4},{7,5},{8,10},{9,11},{10,... | collective-permute-start | bytes 1572872 | tf_op jit(solution)/shard_map/ppermute | solution.py:513
  305.6 117.1 %collective-permute-start.62 = (bf16[256,1024]{1,0:T(8,128)(2,1)S(1)}, bf16[256,1024]{1,0:T(8,128)(2,1)S(1)}, u32[]{:S(2)}, u32[]{:S(2)}) collective-permute-start(bf16[256,1024]{1,0:T(8,128)(2,1)S(1)} %fusion.49), channel_id=1, source_target_pairs={{0,2},{1,3},{2,0},{3,1},{4,6},{5,7},{6,4},{7,5},{8,10},{9,11},{10,... | collective-permute-start | bytes 1572872 | tf_op jit(solution)/shard_map/ppermute | solution.py:513
  328.1 52.3 %collective-permute-start.81 = (bf16[128,1152]{1,0:T(8,128)(2,1)S(1)}, bf16[128,1152]{1,0:T(8,128)(2,1)S(1)}, u32[]{:S(2)}, u32[]{:S(2)}) collective-permute-start(bf16[128,1152]{1,0:T(8,128)(2,1)S(1)} %get-tuple-element.159), channel_id=1, source_target_pairs={{0,8},{4,12},{8,0},{12,4},{16,24},{20,28},{24,16},{28,20},{1,9},{5... | collective-permute-start | bytes 884744 | tf_op jit(solution)/shard_map/ppermute | solution.py:513
  352.9 27.9 %collective-permute-start.83 = (bf16[128,1152]{1,0:T(8,128)(2,1)S(1)}, bf16[128,1152]{1,0:T(8,128)(2,1)S(1)}, u32[]{:S(2)}, u32[]{:S(2)}) collective-permute-start(bf16[128,1152]{1,0:T(8,128)(2,1)S(1)} %get-tuple-element.160), channel_id=1, source_target_pairs={{0,24},{4,28},{8,16},{12,20},{16,8},{20,12},{24,0},{28,4},{1,25},{... | collective-permute-start | bytes 884744 | tf_op jit(solution)/shard_map/ppermute | solution.py:513
  377.5 26.3 %collective-permute-start.82 = (bf16[128,1152]{1,0:T(8,128)(2,1)S(1)}, bf16[128,1152]{1,0:T(8,128)(2,1)S(1)}, u32[]{:S(2)}, u32[]{:S(2)}) collective-permute-start(bf16[128,1152]{1,0:T(8,128)(2,1)S(1)} %get-tuple-element.161), channel_id=1, source_target_pairs={{0,16},{4,20},{8,24},{12,28},{16,0},{20,4},{24,8},{28,12},{1,17},{... | collective-permute-start | bytes 884744 | tf_op jit(solution)/shard_map/ppermute | solution.py:513
  380.4 23.6 %collective-permute-start.77 = (bf16[128,1152]{1,0:T(8,128)(2,1)S(1)}, bf16[128,1152]{1,0:T(8,128)(2,1)S(1)}, u32[]{:S(2)}, u32[]{:S(2)}) collective-permute-start(bf16[128,1152]{1,0:T(8,128)(2,1)S(1)} %get-tuple-element.156), channel_id=1, source_target_pairs={{0,8},{4,12},{8,0},{12,4},{16,24},{20,28},{24,16},{28,20},{1,9},{5... | collective-permute-start | bytes 884744 | tf_op jit(solution)/shard_map/ppermute | solution.py:513
  380.8 24.7 %collective-permute-start.79 = (bf16[128,1152]{1,0:T(8,128)(2,1)S(1)}, bf16[128,1152]{1,0:T(8,128)(2,1)S(1)}, u32[]{:S(2)}, u32[]{:S(2)}) collective-permute-start(bf16[128,1152]{1,0:T(8,128)(2,1)S(1)} %get-tuple-element.157), channel_id=1, source_target_pairs={{0,24},{4,28},{8,16},{12,20},{16,8},{20,12},{24,0},{28,4},{1,25},{... | collective-permute-start | bytes 884744 | tf_op jit(solution)/shard_map/ppermute | solution.py:513
  403.9 25.4 %collective-permute-start.51 = (bf16[256,1024]{1,0:T(8,128)(2,1)S(1)}, bf16[256,1024]{1,0:T(8,128)(2,1)S(1)}, u32[]{:S(2)}, u32[]{:S(2)}) collective-permute-start(bf16[256,1024]{1,0:T(8,128)(2,1)S(1)} %fusion.45), channel_id=1, source_target_pairs={{0,2},{1,3},{2,0},{3,1},{4,6},{5,7},{6,4},{7,5},{8,10},{9,11},{10,... | collective-permute-start | bytes 1572872 | tf_op jit(solution)/shard_map/ppermute | solution.py:513
  422.7 28.0 %collective-permute-start.74 = (bf16[128,1152]{1,0:T(8,128)(2,1)S(1)}, bf16[128,1152]{1,0:T(8,128)(2,1)S(1)}, u32[]{:S(2)}, u32[]{:S(2)}) collective-permute-start(bf16[128,1152]{1,0:T(8,128)(2,1)S(1)} %get-tuple-element.155), channel_id=1, source_target_pairs={{0,16},{4,20},{8,24},{12,28},{16,0},{20,4},{24,8},{28,12},{1,17},{... | collective-permute-start | bytes 884744 | tf_op jit(solution)/shard_map/ppermute | solution.py:513
  452.8 43.4 %collective-permute-start.56 = (bf16[256,1024]{1,0:T(8,128)(2,1)}, bf16[256,1024]{1,0:T(8,128)(2,1)S(1)}, u32[]{:S(2)}, u32[]{:S(2)}) collective-permute-start(bf16[256,1024]{1,0:T(8,128)(2,1)} %get-tuple-element.135.refs_4_), channel_id=1, source_target_pairs={{0,1},{1,0},{2,3},{3,2},{4,5},{5,4},{6,7},{7,6},{8,9},{9,8},{10,11... | collective-permute-start | bytes 1572872 | tf_op jit(solution)/shard_map/ppermute | solution.py:513
  465.5 30.7 %collective-permute-start.58 = (bf16[256,1024]{1,0:T(8,128)(2,1)S(1)}, bf16[256,1024]{1,0:T(8,128)(2,1)S(1)}, u32[]{:S(2)}, u32[]{:S(2)}) collective-permute-start(bf16[256,1024]{1,0:T(8,128)(2,1)S(1)} %collective-permute-done.57.refs_6_), channel_id=1, source_target_pairs={{0,1},{1,0},{2,3},{3,2},{4,5},{5,4},{6,7},{7,6},{8,9},{9,8},{10,11... | collective-permute-start | bytes 1572872 | tf_op jit(solution)/shard_map/ppermute | solution.py:513
  534.8 18.7 %collective-permute-start.68 = (bf16[4,128,768]{2,1,0:T(8,128)(2,1)}, bf16[4,128,768]{2,1,0:T(8,128)(2,1)}, u32[]{:S(2)}, u32[]{:S(2)}) collective-permute-start(bf16[4,128,768]{2,1,0:T(8,128)(2,1)} %add_convert_fusion), channel_id=1, source_target_pairs={{0,4},{4,0},{8,12},{12,8},{16,20},{20,16},{24,28},{28,24},{1,5},{5... | collective-permute-start | bytes 2359304 | tf_op jit(solution)/shard_map/ppermute | solution.py:513
  535.4 19.7 %collective-permute-start.59 = (bf16[2,256,1024]{2,1,0:T(8,128)(2,1)}, bf16[2,256,1024]{2,1,0:T(8,128)(2,1)}, u32[]{:S(2)}, u32[]{:S(2)}) collective-permute-start(bf16[2,256,1024]{2,1,0:T(8,128)(2,1)} %get-tuple-element.80), channel_id=1, source_target_pairs={{0,1},{1,0},{2,3},{3,2},{4,5},{5,4},{6,7},{7,6},{8,9},{9,8},{10,11... | collective-permute-start | bytes 3145736 | tf_op jit(solution)/shard_map/ppermute | solution.py:513
  556.4 20.6 %collective-permute-start.60 = (bf16[256,1024]{1,0:T(8,128)(2,1)S(1)}, bf16[256,1024]{1,0:T(8,128)(2,1)S(1)}, u32[]{:S(2)}, u32[]{:S(2)}) collective-permute-start(bf16[256,1024]{1,0:T(8,128)(2,1)S(1)} %fusion.48), channel_id=1, source_target_pairs={{0,2},{1,3},{2,0},{3,1},{4,6},{5,7},{6,4},{7,5},{8,10},{9,11},{10,... | collective-permute-start | bytes 1572872 | tf_op jit(solution)/shard_map/ppermute | solution.py:513
  558.2 21.3 %collective-permute-start.67 = (bf16[256,1024]{1,0:T(8,128)(2,1)S(1)}, bf16[256,1024]{1,0:T(8,128)(2,1)S(1)}, u32[]{:S(2)}, u32[]{:S(2)}) collective-permute-start(bf16[256,1024]{1,0:T(8,128)(2,1)S(1)} %fusion.50), channel_id=1, source_target_pairs={{0,2},{1,3},{2,0},{3,1},{4,6},{5,7},{6,4},{7,5},{8,10},{9,11},{10,... | collective-permute-start | bytes 1572872 | tf_op jit(solution)/shard_map/ppermute | solution.py:513
  (127 other events, 1467.6 us)

commit v2 on v1

--- a/solution.py
+++ b/solution.py
@@ -2,6 +2,7 @@
 
 import jax
 import jax.numpy as jnp
+import numpy as np
 from jax import lax
 from jax.experimental import pallas as pl
 from jax.experimental.pallas import tpu as pltpu
@@ -86,6 +87,80 @@
         (send_ref if slot % 2 else keep_ref)[slot // 2] = whole[rows_of(me ^ slot, size), :]
 
 
+def padded_heads(first, second, low, g, e):
+    here = low if e == 0 else jnp.logical_not(low)
+    return jnp.where(here, first if g == e else second, 0.0).astype(BF16)
+
+
+def project_rows(r, size, length, xs, ws, tabs, gains, raw_ref, q_ref, k_ref, v_ref, kp, vp):
+    rows = rows_of(r, size)
+    cos_ref, sin_ref = tabs
+    gq_ref, gk_ref = gains
+    mean_of = head_blocks(1.0 / 64)
+    low = low_half((size, LANES))
+    projected = dot(xs[rows, :], ws[:, :512])
+    raw_ref[rows, :] = projected[:, :384]
+    cosines, sines = cos_ref[rows, :], sin_ref[rows, :]
+
+    def turned(values, gain):
+        mean = dot(values * values, mean_of, precision=HIGH)
+        normed = values * lax.rsqrt(mean + EPS) * gain
+        return normed * cosines + partner(normed) * sines
+
+    for g in range(2):
+        lanes = slice(LANES * g, LANES * (g + 1))
+        q_ref[rows, lanes] = turned(projected[:, lanes], gq_ref[...]).astype(BF16)
+    keys = turned(projected[:, 256:384], gk_ref[...])
+    values = projected[:, 384:512]
+    k_ref[rows, :] = keys.astype(BF16)
+    v_ref[rows, :] = values.astype(BF16)
+    live = r * size + iota((size, LANES), 0) < length
+    ones = jnp.where(live, 1.0, 0.0)
+    values = jnp.where(live, values, 0.0)
+    keys_swap, values_swap = pltpu.roll(keys, 64, 1), pltpu.roll(values, 64, 1)
+    for g in range(2):
+        for e in range(2):
+            kp[2 * g + e, rows, :] = padded_heads(keys, keys_swap, low, g, e)
+            vp[2 * g + e, rows, :LANES] = padded_heads(values, values_swap, low, g, e)
+            vp[2 * g + e, rows, LANES:] = padded_heads(ones, ones, low, g, e)
+
+
+def attend_rows(i, size, q_ref, kp, vp, acc, att_ref, lse_ref):
+    rows = rows_of(i, size)
+    factor = LOG2E / 8.0
+    causal = iota((size, size), 1) <= iota((size, size), 0)
+    queries = [q_ref[rows, LANES * g : LANES * (g + 1)] for g in range(2)]
+
+    def block(kb, masked):
+        cols = rows_of(kb, size)
+        sums = []
+        for g in range(2):
+            total = None
+            for e in range(2):
+                weights = jnp.exp2(dot_nt(queries[g], kp[2 * g + e, cols, :]) * factor)
+                if masked:
+                    weights = jnp.where(causal, weights, 0.0)
+                part = dot(weights.astype(BF16), vp[2 * g + e, cols, :])
+                total = part if total is None else total + part
+            sums.append(total)
+        return sums
+
+    for g, total in enumerate(block(i, True)):
+        acc[g] = total
+
+    def more(kb, carry):
+        for g, total in enumerate(block(kb, False)):
+            acc[g] += total
+        return carry
+
+    lax.fori_loop(0, i, more, 0)
+    for g in range(2):
+        lanes = slice(LANES * g, LANES * (g + 1))
+        summed = acc[g, :, LANES:]
+        att_ref[rows, lanes] = (acc[g, :, :LANES] / summed).astype(BF16)
+        lse_ref[rows, lanes] = jnp.log2(summed)
+
+
 def attn_fwd_kernel(parts, n_w, scal, cos_ref, sin_ref, gq_ref, gk_ref, *refs):
     x_refs, refs = refs[:parts], refs[parts:]
     w_refs, refs = refs[:n_w], refs[n_w:]
@@ -96,77 +171,18 @@
     copies += load_all(x_refs, [xs.at[rows_of(me_t ^ j, size)] for j in range(parts)], sems, n_w)
     for copy in copies:
         copy.wait()
-    mean_of = head_blocks(1.0 / 64)
-    low = low_half((size, LANES))
-    factor = LOG2E / 8.0
 
     def project(r, carry):
-        rows = rows_of(r, size)
-        projected = dot(xs[rows, :], ws[:, :512])
-        raw_ref[rows, :] = projected[:, :384]
-        cosines, sines = cos_ref[rows, :], sin_ref[rows, :]
-
-        def turned(values, gain):
-            mean = dot(values * values, mean_of, precision=HIGH)
-            normed = values * lax.rsqrt(mean + EPS) * gain
-            return normed * cosines + partner(normed) * sines
-
-        for g in range(2):
-            lanes = slice(LANES * g, LANES * (g + 1))
-            q_ref[rows, lanes] = turned(projected[:, lanes], gq_ref[...]).astype(BF16)
-        keys = turned(projected[:, 256:384], gk_ref[...])
-        values = projected[:, 384:512]
-        k_ref[rows, :] = keys.astype(BF16)
-        v_ref[rows, :] = values.astype(BF16)
-        live = r * size + iota((size, LANES), 0) < length
-        ones = jnp.where(live, 1.0, 0.0)
-        values = jnp.where(live, values, 0.0)
-        keys_swap, values_swap = pltpu.roll(keys, 64, 1), pltpu.roll(values, 64, 1)
-        for g in range(2):
-            for e in range(2):
-                here = low if e == 0 else jnp.logical_not(low)
-                kp[2 * g + e, rows, :] = jnp.where(here, keys if g == e else keys_swap, 0.0).astype(BF16)
-                vp[2 * g + e, rows, :LANES] = jnp.where(here, values if g == e else values_swap, 0.0).astype(BF16)
-                vp[2 * g + e, rows, LANES:] = jnp.where(here, ones, 0.0).astype(BF16)
+        project_rows(
+            r, size, length, xs, ws, (cos_ref, sin_ref), (gq_ref, gk_ref), raw_ref, q_ref, k_ref, v_ref, kp, vp
+        )
         return carry
 
+    def attend(i, carry):
+        attend_rows(i, size, q_ref, kp, vp, acc, att_ref, lse_ref)
+        return carry
+
     lax.fori_loop(0, parts, project, 0)
-    causal = iota((size, size), 1) <= iota((size, size), 0)
-
-    def attend(i, carry):
-        rows = rows_of(i, size)
-        queries = [q_ref[rows, LANES * g : LANES * (g + 1)] for g in range(2)]
-
-        def block(kb, masked):
-            cols = rows_of(kb, size)
-            sums = []
-            for g in range(2):
-                total = None
-                for e in range(2):
-                    weights = jnp.exp2(dot_nt(queries[g], kp[2 * g + e, cols, :]) * factor)
-                    if masked:
-                        weights = jnp.where(causal, weights, 0.0)
-                    part = dot(weights.astype(BF16), vp[2 * g + e, cols, :])
-                    total = part if total is None else total + part
-                sums.append(total)
-            return sums
-
-        for g, total in enumerate(block(i, True)):
-            acc[g] = total
-
-        def more(kb, carry):
-            for g, total in enumerate(block(kb, False)):
-                acc[g] += total
-            return carry
-
-        lax.fori_loop(0, i, more, 0)
-        for g in range(2):
-            lanes = slice(LANES * g, LANES * (g + 1))
-            summed = acc[g, :, LANES:]
-            att_ref[rows, lanes] = (acc[g, :, :LANES] / summed).astype(BF16)
-            lse_ref[rows, lanes] = jnp.log2(summed)
-        return carry
-
     lax.fori_loop(0, parts, attend, 0)
     for j in range(parts):
         out = dot_nt(att_ref[rows_of(me_t ^ j, size), :], ws[:, 512:])
@@ -509,6 +525,337 @@
     )(scal, *hids, *ggus, *[shard for chunk in w_chunks for shard in chunk])
 
 
+def flip(index, bits):
+    for bit in (1, 2, 4):
+        if bits & bit:
+            index = index + bit - 2 * bit * lax.rem(lax.div(index, bit), 2)
+    return index
+
+
+def enter(me_d, me_t):
+    barrier = pltpu.get_barrier_semaphore()
+    devices = [{"dp": flip(me_d, bits)} for bits in (1, 2, 4, 6)]
+    devices += [{"tensor": flip(me_t, bits)} for bits in (1, 2)]
+    for device in devices:
+        pl.semaphore_signal(barrier, inc=1, device_id=device, device_id_type=pl.DeviceIdType.MESH)
+    return lambda: pl.semaphore_wait(barrier, len(devices))
+
+
+def remote(source, target, sems, number, device):
+    return pltpu.make_async_remote_copy(
+        src_ref=source,
+        dst_ref=target,
+        send_sem=sems.at[0, number],
+        recv_sem=sems.at[1, number],
+        device_id=device,
+        device_id_type=pl.DeviceIdType.MESH,
+    )
+
+
+class ShardGather:
+    COPIES = 7
+
+    def __init__(self, shard, whole, sems, first, me_d):
+        size = shard.shape[0]
+        mine = whole.at[rows_of(me_d, size)]
+        beside = {"dp": flip(me_d, 1)}
+        self.own = [
+            remote(shard, mine, sems, first + n, {"dp": flip(me_d, bits)})
+            for n, bits in enumerate((1, 2, 4, 6))
+        ]
+        self.passed = []
+        for n, bits in enumerate((2, 4, 6)):
+            there = whole.at[rows_of(flip(me_d, bits), size)]
+            self.passed.append(remote(there, there, sems, first + 4 + n, beside))
+
+    def start(self):
+        for copy in self.own:
+            copy.start()
+
+    def forward(self):
+        for come, onward in zip(self.own[1:], self.passed):
+            come.wait_recv()
+            onward.start()
+
+    def arrive(self):
+        self.own[0].wait_recv()
+        for copy in self.passed:
+            copy.wait_recv()
+
+    def drain(self):
+        for copy in self.own + self.passed:
+            copy.wait_send()
+
+
+class TokenGather:
+    COPIES = 3
+
+    def __init__(self, block, whole, sems, first, me_t):
+        size = block.shape[0]
+        mine = whole.at[rows_of(me_t, size)]
+        there = whole.at[rows_of(flip(me_t, 2), size)]
+        near = {"tensor": flip(me_t, 1)}
+        self.near = remote(block, mine, sems, first, near)
+        self.far = remote(block, mine, sems, first + 1, {"tensor": flip(me_t, 2)})
+        self.passed = remote(there, there, sems, first + 2, near)
+
+    def start(self):
+        self.far.start()
+        self.near.start()
+
+    def forward(self):
+        self.far.wait_recv()
+        self.passed.start()
+
+    def arrive(self):
+        self.near.wait_recv()
+        self.passed.wait_recv()
+
+    def drain(self):
+        for copy in (self.near, self.far, self.passed):
+            copy.wait_send()
+
+
+class TokenReduce:
+    COPIES = 3
+
+    def __init__(self, blocks, near, far, sems, first, me_t):
+        device = {"tensor": flip(me_t, 1)}
+        self.blocks, self.near_ref, self.far_ref = blocks, near, far
+        self.me = me_t
+        self.across = flip(me_t, 2)
+        self.near = [
+            remote(blocks.at[flip(me_t, 1 + 2 * n)], near.at[n], sems, first + n, device) for n in range(2)
+        ]
+        self.far = remote(near.at[1], far, sems, first + 2, {"tensor": flip(me_t, 2)})
+
+    def start(self, n):
+        self.near[n].start()
+
+    def middle(self):
+        self.near[1].wait_recv()
+
+        def step(b, carry):
+            rows = rows_of(b, 32)
+            total = self.blocks[self.across, rows, :].astype(F32) + self.near_ref[1, rows, :].astype(F32)
+            self.near_ref[1, rows, :] = total.astype(BF16)
+            return carry
+
+        lax.fori_loop(0, self.near_ref.shape[1] // 32, step, 0)
+        self.far.start()
+
+    def arrive(self):
+        self.near[0].wait_recv()
+        self.far.wait_recv()
+
+    def rows(self, rows):
+        total = self.blocks[self.me, rows, :].astype(F32) + self.near_ref[0, rows, :].astype(F32)
+        return total + self.far_ref[rows, :].astype(F32)
+
+    def drain(self):
+        for copy in self.near + [self.far]:
+            copy.wait_send()
+
+
+def by_rows(count, step, body):
+    def run(b, carry):
+        body(rows_of(b, step))
+        return carry
+
+    lax.fori_loop(0, count // step, run, 0)
+
+
+def rms_factor(values):
+    return lax.rsqrt(jnp.mean(values * values, axis=-1, keepdims=True) + EPS)
+
+
+def forward_kernel(
+    lengths, x_ref, aw_ref, up_ref, fw_ref, cos_ref, sin_ref, gq_ref, gk_ref, mg_ref, dg_ref,
+    aw_out, fw_out, normed_out, up_out, dense_out, resid_ref, raw_ref, q_ref, k_ref, v_ref, att_ref, lse_ref,
+    xs, ws, kp, vp, acc, outp, near, far, dense, sems, local_sems,
+):
+    seqs, size, width = resid_ref.shape
+    parts = xs.shape[1] // size
+    n_c = fw_ref.shape[0]
+    me_t, me_d = lax.axis_index("tensor"), lax.axis_index("dp")
+    entered = enter(me_d, me_t)
+    mine_t, mine_d = rows_of(me_t, size), rows_of(me_d, aw_ref.shape[0])
+
+    first = 0
+    attn_w = ShardGather(aw_ref, ws, sems, first, me_d)
+    first += ShardGather.COPIES
+    ff_w = []
+    for c in range(n_c):
+        ff_w.append(ShardGather(fw_ref.at[c], fw_out.at[c], sems, first, me_d))
+        first += ShardGather.COPIES
+    normed, ups, denses, outs = [], [], [], []
+    for s in range(seqs):
+        normed.append(TokenGather(xs.at[s, mine_t], xs.at[s], sems, first, me_t))
+        ups.append(TokenGather(up_ref.at[s], up_out.at[s], sems, first + 3, me_t))
+        denses.append(TokenGather(dense.at[s], dense_out.at[s], sems, first + 6, me_t))
+        outs.append(TokenReduce(outp.at[s], near.at[s], far.at[s], sems, first + 9, me_t))
+        first += 12
+
+    def here(source, target, number):
+        copy = pltpu.make_async_copy(source, target, local_sems.at[number])
+        copy.start()
+        return copy
+
+    mine = here(aw_ref, ws.at[mine_d], 0)
+    stays = [here(up_ref.at[s], up_out.at[s, mine_t], 1 + s) for s in range(seqs)]
+    stays += [here(fw_ref.at[c], fw_out.at[c, mine_d], 1 + seqs + c) for c in range(n_c)]
+    used = 1 + seqs + n_c
+
+    for s in range(seqs):
+
+        def norm(rows):
+            values = x_ref[rows, width * s : width * (s + 1)].astype(F32)
+            target = pl.ds(pl.multiple_of(me_t * size + rows.start, 32), 32)
+            xs[s, target, :] = (values * rms_factor(values) * mg_ref[...]).astype(BF16)
+
+        by_rows(size, 32, norm)
+    entered()
+    normed[0].start()
+    attn_w.start()
+    normed[1].start()
+    attn_w.forward()
+    normed[0].forward()
+    normed[0].arrive()
+    mine.wait()
+    attn_w.arrive()
+    ff_w[0].start()
+    stays.append(here(ws, aw_out, used))
+    used += 1
+
+    def project(s):
+        def run(r, carry):
+            project_rows(
+                r, size, lengths[s], xs.at[s], ws, (cos_ref, sin_ref), (gq_ref, gk_ref),
+                raw_ref.at[s], q_ref.at[s], k_ref.at[s], v_ref.at[s], kp, vp,
+            )
+            return carry
+
+        lax.fori_loop(0, parts, run, 0)
+
+    def attend(s, start, stop):
+        def run(i, carry):
+            attend_rows(i, size, q_ref.at[s], kp, vp, acc, att_ref.at[s], lse_ref.at[s])
+            return carry
+
+        lax.fori_loop(start, stop, run, 0)
+
+    def out(s):
+        for n, bits in enumerate((1, 3, 2, 0)):
+            block = flip(me_t, bits)
+            result = dot_nt(att_ref[s, rows_of(block, size), :], ws[:, 512:])
+            outp[s, block] = result.astype(BF16)
+            if n < 2:
+                outs[s].start(n)
+
+    def after(s):
+        outs[s].arrive()
+
+        def norm(rows):
+            values = x_ref[rows, width * s : width * (s + 1)].astype(F32) + outs[s].rows(rows)
+            resid_ref[s, rows, :] = values
+            dense[s, rows, :] = (values * rms_factor(values) * dg_ref[...]).astype(BF16)
+
+        by_rows(size, 32, norm)
+        denses[s].start()
+        stays.append(here(dense.at[s], dense_out.at[s, mine_t], used + s))
+
+    project(0)
+    normed[1].forward()
+    for s in range(seqs):
+        ups[s].start()
+    attend(0, 0, 3)
+    ff_w[0].forward()
+    if n_c > 1:
+        ff_w[1].start()
+    attend(0, 3, parts)
+    out(0)
+    normed[1].arrive()
+    for s in range(seqs):
+        ups[s].forward()
+    outs[0].middle()
+    project(1)
+    attend(1, 0, 3)
+    after(0)
+    attend(1, 3, parts)
+    out(1)
+    outs[1].middle()
+    denses[0].forward()
+    for c in range(1, n_c):
+        ff_w[c].forward()
+        if c + 1 < n_c:
+            ff_w[c + 1].start()
+    after(1)
+    denses[1].forward()
+    used += seqs
+    stays += [here(xs.at[s], normed_out.at[s], used + s) for s in range(seqs)]
+    for c in range(n_c):
+        ff_w[c].arrive()
+    for s in range(seqs):
+        ups[s].arrive()
+        denses[s].arrive()
+    for copy in stays:
+        copy.wait()
+    attn_w.drain()
+    for exchange in ff_w + normed + ups + denses + outs:
+        exchange.drain()
+
+
+def fused_forward(lengths, x, aw, up, fw, tabs, gains):
+    seqs, size, width = up.shape
+    parts = 4
+    full = parts * size
+    shard, cols = aw.shape
+    n_c, _, wide = fw.shape
+    dp = 8
+
+    def shape(dims, kind):
+        return jax.ShapeDtypeStruct(dims, kind)
+
+    n_sems = ShardGather.COPIES * (1 + n_c) + 12 * seqs
+    return pl.pallas_call(
+        forward_kernel,
+        out_shape=(
+            shape((dp * shard, cols), BF16),
+            shape((n_c, dp * shard, wide), BF16),
+            shape((seqs, full, width), BF16),
+            shape((seqs, full, width), BF16),
+            shape((seqs, full, width), BF16),
+            shape((seqs, size, width), F32),
+            shape((seqs, full, 384), F32),
+            shape((seqs, full, 256), BF16),
+            shape((seqs, full, 128), BF16),
+            shape((seqs, full, 128), BF16),
+            shape((seqs, full, 256), BF16),
+            shape((seqs, full, 256), F32),
+        ),
+        in_specs=[SMEM, VMEM] + [ANY] * 3 + [VMEM] * 6,
+        out_specs=(ANY,) * 5 + (VMEM,) * 7,
+        scratch_shapes=[
+            pltpu.VMEM((seqs, full, width), BF16),
+            pltpu.VMEM((dp * shard, cols), BF16),
+            pltpu.VMEM((4, full, LANES), BF16),
+            pltpu.VMEM((4, full, 2 * LANES), BF16),
+            pltpu.VMEM((2, size, 2 * LANES), F32),
+            pltpu.VMEM((seqs, parts, size, width), BF16),
+            pltpu.VMEM((seqs, 2, size, width), BF16),
+            pltpu.VMEM((seqs, size, width), BF16),
+            pltpu.VMEM((seqs, size, width), BF16),
+            pltpu.SemaphoreType.DMA((2, n_sems)),
+            pltpu.SemaphoreType.DMA((2 + 3 * seqs + n_c,)),
+        ],
+        compiler_params=pltpu.CompilerParams(
+            vmem_limit_bytes=VMEM_LIMIT, collective_id=0, has_side_effects=True
+        ),
+        cost_estimate=pl.CostEstimate(flops=16_000_000_000, bytes_accessed=40_000_000, transcendentals=6_000_000),
+        name="forward",
+    )(lengths, x, aw, up, fw, *tabs, *gains)
+
+
 def swap(values, axis, bits):
     return lax.ppermute(values, axis, [(i, i ^ bits) for i in range(lax.axis_size(axis))])
 
@@ -575,7 +922,7 @@
     return (jnp.tile(cosines, (1, 4)), jnp.tile(jnp.concatenate([-sines, sines], axis=1), (1, 2)))
 
 
-def local(
+def local_plain(
     inputs,
     lengths,
     query_weight,
@@ -640,6 +987,151 @@
         seconds.append(factor)
         dense.append(gather_tokens(dense_in.astype(BF16)))
 
+    x_parts = [part for s in range(seqs) for part in dense[s]]
+    u_parts = [part for s in range(seqs) for part in up_parts[s]]
+    hids, ggus, ff_grads = [], [], []
+    for c in range(n_c):
+        hid, ggu, grads = feed_forward(scals[0], x_parts, u_parts, ff_w[c])
+        hids.append(hid)
+        ggus.append(ggu)
+        ff_grads.append(scatter_shards(grads))
+
+    block_out, input_gradient, attn_grads = [], [], []
+    mixer_part = dense_part = gain_part = 0.0
+    for s in range(seqs):
+        ykeep, ysend, gkeep, gsend = ff_out(s, scals[s], parts, size, hids, ggus, ff_w)
+        grad_dense = scatter_tokens(gkeep, gsend)
+        dense_part = dense_part + jnp.sum(grad_dense * residual[s] * seconds[s], axis=0)
+        grad_residual = upstream[s] + norm_back(residual[s], seconds[s], dense_gain, grad_dense)
+        r_parts = gather_tokens(grad_residual.astype(BF16))
+        nkeep, nsend, gains, grads = attn_bwd(
+            scals[s], cosines, sines, gq, gk, saved[s], normed[s], r_parts, attn_w
+        )
+        attn_grads.append(grads)
+        gain_part = gain_part + gains
+        grad_normed = scatter_tokens(nkeep, nsend)
+        factor = firsts[s][1]
+        mixer_part = mixer_part + jnp.sum(grad_normed * tokens[s] * factor, axis=0)
+        input_gradient.append(grad_residual + norm_back(tokens[s], factor, mixer_gain, grad_normed))
+        out_sum = scatter_tokens(ykeep, ysend)
+        block_out.append(jnp.where(valid[s], residual[s] + out_sum, 0.0).astype(BF16))
+
+    summed = [
+        sum(part.astype(F32) for part in parts_of).astype(BF16) for parts_of in zip(*attn_grads)
+    ]
+    attn_grad = scatter_shards(summed)
+    early = sum_everywhere(jnp.concatenate([dense_part.reshape(-1, LANES), gain_part], axis=0))
+    mixer = sum_everywhere(mixer_part.reshape(-1, LANES)).reshape(-1)
+    dense_rows = width // LANES
+    folded = early[dense_rows:, :head] + early[dense_rows:, head:]
+    inner_gradient = jnp.stack(
+        [
+            jnp.concatenate([grad[:, p * cols : (p + 1) * cols] for grad in ff_grads], axis=1)
+            for p in range(2)
+        ],
+        axis=1,
+    )
+    down_gradient = jnp.concatenate([grad[:, 2 * cols :] for grad in ff_grads], axis=1).T
+    return (
+        jnp.stack(block_out, axis=1),
+        jnp.stack(input_gradient, axis=1),
+        attn_grad[:, :query_cols],
+        attn_grad[:, query_cols : query_cols + 2 * pair_cols].reshape(shard, 2, pair_cols),
+        attn_grad[:, query_cols + 2 * pair_cols :].T,
+        inner_gradient,
+        down_gradient,
+        mixer,
+        folded[0],
+        folded[1],
+        early[:dense_rows].reshape(-1),
+    )
+
+
+def local(*args):
+    inputs, shard = args[0], args[2].shape[0]
+    if lax.axis_size("dp") == 8 and lax.axis_size("tensor") == 4 and shard % LANES == 0:
+        return local_fused(*args)
+    return local_plain(*args)
+
+
+def rope_tables(full, head):
+    half = head // 2
+    freqs = np.float32(THETA) ** (-np.arange(half, dtype=np.float32) * np.float32(2.0) / np.float32(head))
+    angles = np.arange(full, dtype=np.float32)[:, None] * freqs[None, :].astype(np.float32)
+    cosines, sines = np.cos(angles), np.sin(angles)
+    return (
+        jnp.asarray(np.tile(cosines, (1, 4)), F32),
+        jnp.asarray(np.tile(np.concatenate([-sines, sines], axis=1), (1, 2)), F32),
+    )
+
+
+def local_fused(
+    inputs,
+    lengths,
+    query_weight,
+    key_value_weight,
+    output_weight,
+    inner_weight,
+    down_weight,
+    mixer_gain,
+    query_gain,
+    key_gain,
+    dense_gain,
+    cotangent,
+):
+    size, seqs, width = inputs.shape
+    parts = lax.axis_size("tensor")
+    full = size * parts
+    head = query_gain.shape[0]
+    query_cols = query_weight.shape[1]
+    pair_cols = key_value_weight.shape[2]
+    hidden = inner_weight.shape[2]
+    shard = query_weight.shape[0]
+    me_t, me_d = lax.axis_index("tensor"), lax.axis_index("dp")
+    n_c = 3
+    cols = hidden // n_c
+    tabs = rope_tables(full, head)
+    gq = jnp.tile(query_gain, 2)[None, :]
+    gk = jnp.tile(key_gain, 2)[None, :]
+    gains = (gq, gk, mixer_gain[None, :], dense_gain[None, :])
+    down_turned = down_weight.T
+    attn_shard = jnp.concatenate(
+        [query_weight, key_value_weight.reshape(shard, 2 * pair_cols), output_weight.T], axis=1
+    )
+    ff_shard = jnp.stack(
+        [
+            jnp.concatenate(
+                [inner_weight[:, 0, part], inner_weight[:, 1, part], down_turned[:, part]], axis=1
+            )
+            for part in (slice(c * cols, (c + 1) * cols) for c in range(n_c))
+        ]
+    )
+    positions = me_t * size + jnp.arange(size, dtype=jnp.int32)
+    valid = [(positions < lengths[s])[:, None] for s in range(seqs)]
+    upstream = jnp.stack([jnp.where(valid[s], cotangent[:, s], 0) for s in range(seqs)])
+    x = inputs.reshape(size, seqs * width)
+
+    (aw, fw, normed, ups, dense, resid, *saved) = fused_forward(
+        lengths, x, attn_shard, upstream, ff_shard, tabs, gains
+    )
+    cosines, sines = tabs
+    scals = [
+        jnp.stack([me_t.astype(jnp.int32), me_d.astype(jnp.int32), lengths[s], jnp.int32(0)])
+        for s in range(seqs)
+    ]
+    def sl(a,n,me,cnt):
+        return [lax.dynamic_slice_in_dim(a,(me^j)*n,n,0) for j in range(cnt)]
+    attn_w=sl(aw,shard,me_d,8)
+    ff_w=[sl(fw[c],shard,me_d,8) for c in range(n_c)]
+    tokens = [inputs[:, s].astype(F32) for s in range(seqs)]
+    normed=[sl(normed[s],size,me_t,4) for s in range(seqs)]
+    up_parts=[sl(ups[s],size,me_t,4) for s in range(seqs)]
+    dense=[sl(dense[s],size,me_t,4) for s in range(seqs)]
+    residual=[resid[s] for s in range(seqs)]
+    saved=[[a[s] for a in saved] for s in range(seqs)]
+    seconds=[lax.rsqrt(jnp.mean(r*r,axis=-1,keepdims=True)+EPS) for r in residual]
+    firsts=[(None,lax.rsqrt(jnp.mean(r*r,axis=-1,keepdims=True)+EPS)) for r in tokens]
+    upstream=[upstream[s].astype(F32) for s in range(seqs)]
     x_parts = [part for s in range(seqs) for part in dense[s]]
     u_parts = [part for s in range(seqs) for part in up_parts[s]]
     hids, ggus, ff_grads = [], [], []

time: 610 us -> 585 us (0.959)
  waiting for transfers between devices: 241 us -> 118 us
  Pallas kernels: 184 us -> 287 us
  local copies, waits for them, and re-layouts: 39.8 us -> 67 us
  starting transfers between devices: 98.1 us -> 73.8 us
  other arithmetic: 36 us -> 28.5 us
    ppermute x94 -> x44, waiting for transfers between devices: 241 us -> 118 us  [swap(): lax.ppermute(values, axis, [(i, i ^ bits) for i in range(lax.axis_size(ax...]
    pallas_call x2 -> x1, Pallas kernels: 33.5 us -> 136 us  [fused_forward(): pl.pallas_call(forward_kernel, out_shape=(shape((dp * shard, cols), BF16)...]
    ppermute x94 -> x44, starting transfers between devices: 98.1 us -> 73.8 us  [swap(): lax.ppermute(values, axis, [(i, i ^ bits) for i in range(lax.axis_size(ax...]
    dynamic_slice x0 -> x10, local copies, waits for them, and re-layouts: none -> 16.9 us  [sl(): return [lax.dynamic_slice_in_dim(a, (me ^ j) * n, n, 0) for j in range(cnt)]]
    squeeze x4 -> x8, local copies, waits for them, and re-layouts: 1.62 us -> 7.74 us  [the longest x6 7.19 us: local_fused(): saved = [[a[s] for a in saved] for s in range(seqs)]]
    unnamed x170 -> x121, local copies, waits for them, and re-layouts: 17.9 us -> 24 us
    slice x8 -> x12, local copies, waits for them, and re-layouts: 9.42 us -> 13.4 us  [the longest x1 3.98 us: local_fused(): dense = [sl(dense[s], size, me_t, 4) for s in range(seqs)]]
  transfers between devices with their start and end apart: 94 -> 44, of which waited for: 30 -> 20; matrix products, arithmetic and copies ran while one was open for 10% -> 8% of each run, Pallas kernels for 20% -> 18%
where the time goes in v2:
time: 585 us; the launch traced here: 576 us
  Pallas kernels  287 us (49%)
  waiting for transfers between devices  118 us (20%)
  starting transfers between devices  73.8 us (13%)
  local copies, waits for them, and re-layouts  67 us (11%)
  other arithmetic  28.5 us (5%)
    pallas_call x1, Pallas kernels, fused_forward(): pl.pallas_call(forward_kernel, out_shape=(shape((dp * shard, cols), BF16)...  136 us
    ppermute x44, waiting for transfers between devices, swap(): lax.ppermute(values, axis, [(i, i ^ bits) for i in range(lax.axis_size(ax...  118 us
    ppermute x44, starting transfers between devices, swap(): lax.ppermute(values, axis, [(i, i ^ bits) for i in range(lax.axis_size(ax...  73.8 us
    pallas_call x3, Pallas kernels, feed_forward(): pl.pallas_call(functools.partial(ff_kernel, n_x, n_w), out_shape=(jax.Sha...  60.6 us
    pallas_call x2, Pallas kernels, attn_bwd(): pl.pallas_call(functools.partial(attn_bwd_kernel, parts, n_w), out_shape=...  58.9 us
    pallas_call x2, Pallas kernels, ff_out(): pl.pallas_call(functools.partial(ff_out_kernel, parts, n_c, n_w, seq), ou...  31.5 us
    unnamed x121, local copies, waits for them, and re-layouts  24 us
    dynamic_slice x10, local copies, waits for them, and re-layouts, sl(): return [lax.dynamic_slice_in_dim(a, (me ^ j) * n, n, 0) for j in range(cnt)]  16.9 us
  transfers between devices with their start and end apart: 44, of which 20 were waited for; matrix products, arithmetic and copies ran while one was open for 8% of the time, Pallas kernels for 18%

profile of v2, /device:TPU:0, one launch (start us, length us, event | category | flops | bytes accessed | tf_op | source)
XLA Modules:
  0.0 576.3 jit_solution(2282914857960555260)
XLA Ops:
  16.3 136.0 %forward.1 = (bf16[1024,768]{1,0:T(8,128)(2,1)}, bf16[3,1024,1152]{2,1,0:T(8,128)(2,1)}, bf16[2,1024,1024]{2,1,0:T(8,128)(2,1)}, bf16[2,1024,1024]{2,1,0:T(8,128...) custom-call(s32[2]{0:T(128)} %lengths.1, ...), custom_call_target="tpu_custom_call" | custom-call | flops 16000000000 | bytes 40000000 | tf_op jit(solution)/shard_map/forward/pallas_call | solution.py:820
  152.4 4.0 fusion.78
  156.4 3.0 dynamic-slice_bitcast_fusion.16
  160.7 1.6 copy-done.9
  167.0 2.7 fusion.75
  170.9 3.0 dynamic-slice_bitcast_fusion.32
  173.9 20.2 %feed_forward.4 = (bf16[2048,384]{1,0:T(8,128)(2,1)}, bf16[2048,768]{1,0:T(8,128)(2,1)}, bf16[4,128,1152]{2,1,0:T(8,128)(2,1)}, bf16[4,128,1152]{2,1,0:T(8,128)(2,1)}) custom-call(s32[4]{0:T(128)} %pad_add_fusion.1.scal, bf16[256,1024]{1,0:T(8,128)(2,1)} %get-tuple-element.198.refs_0_, bf16[256,1024]{1,0:T(8,128)(2,1)} %get-tuple-element.197.refs_1_, ...), custom_call_target="tpu_custom_call" | custom-call | flops 9663676416 | bytes 20000000 | tf_op jit(solution)/shard_map/feed_forward/pallas_call | solution.py:452
  198.8 20.3 %feed_forward.3 = (bf16[2048,384]{1,0:T(8,128)(2,1)}, bf16[2048,768]{1,0:T(8,128)(2,1)}, bf16[4,128,1152]{2,1,0:T(8,128)(2,1)}, bf16[4,128,1152]{2,1,0:T(8,128)(2,1)}) custom-call(s32[4]{0:T(128)} %pad_add_fusion.1.scal, bf16[256,1024]{1,0:T(8,128)(2,1)} %get-tuple-element.198.refs_0_, bf16[256,1024]{1,0:T(8,128)(2,1)} %get-tuple-element.197.refs_1_, ...), custom_call_target="tpu_custom_call" | custom-call | flops 9663676416 | bytes 20000000 | tf_op jit(solution)/shard_map/feed_forward/pallas_call | solution.py:452
  219.0 20.2 %feed_forward.5 = (bf16[2048,384]{1,0:T(8,128)(2,1)}, bf16[2048,768]{1,0:T(8,128)(2,1)}, bf16[4,128,1152]{2,1,0:T(8,128)(2,1)}, bf16[4,128,1152]{2,1,0:T(8,128)(2,1)}) custom-call(s32[4]{0:T(128)} %pad_add_fusion.1.scal, bf16[256,1024]{1,0:T(8,128)(2,1)} %get-tuple-element.198.refs_0_, bf16[256,1024]{1,0:T(8,128)(2,1)} %get-tuple-element.197.refs_1_, ...), custom_call_target="tpu_custom_call" | custom-call | flops 9663676416 | bytes 20000000 | tf_op jit(solution)/shard_map/feed_forward/pallas_call | solution.py:452
  239.3 15.7 %feed_forward_out.3 = (bf16[2,256,1024]{2,1,0:T(8,128)(2,1)}, bf16[2,256,1024]{2,1,0:T(8,128)(2,1)}, bf16[2,256,1024]{2,1,0:T(8,128)(2,1)}, bf16[2,256,1024]{2,1,0:T(8,128)(2,1)}) custom-call(s32[4]{0:T(128)} %pad_add_fusion.scal, bf16[2048,384]{1,0:T(8,128)(2,1)} %get-tuple-element.57.refs_0_, bf16[2048,384]{1,0:T(8,128)(2,1)} %get-tuple-element.58.refs_1_, ...), custom_call_target="tpu_custom_call" | custom-call | flops 7247757312 | bytes 22000000 | tf_op jit(solution)/shard_map/feed_forward_out/pallas_call | solution.py:511
  255.5 15.8 %feed_forward_out.2 = (bf16[2,256,1024]{2,1,0:T(8,128)(2,1)}, bf16[2,256,1024]{2,1,0:T(8,128)(2,1)}, bf16[2,256,1024]{2,1,0:T(8,128)(2,1)}, bf16[2,256,1024]{2,1,0:T(8,128)(2,1)}) custom-call(s32[4]{0:T(128)} %pad_add_fusion.1.scal, bf16[2048,384]{1,0:T(8,128)(2,1)} %get-tuple-element.57.refs_0_, bf16[2048,384]{1,0:T(8,128)(2,1)} %get-tuple-element.58.refs_1_, ...), custom_call_target="tpu_custom_call" | custom-call | flops 7247757312 | bytes 22000000 | tf_op jit(solution)/shard_map/feed_forward_out/pallas_call | solution.py:511
  279.0 1.9 slice_bitcast_fusion.1
  289.9 1.7 collective-permute-start.22
  292.5 2.9 collective-permute-start.3
  297.6 6.4 %collective-permute-start.27 = (bf16[128,1152]{1,0:T(8,128)(2,1)S(1)}, bf16[128,1152]{1,0:T(8,128)(2,1)S(1)}, u32[]{:S(2)}, u32[]{:S(2)}) collective-permute-start(bf16[128,1152]{1,0:T(8,128)(2,1)S(1)} %get-tuple-element.210), channel_id=1, source_target_pairs={{0,8},{4,12},{8,0},{12,4},{16,24},{20,28},{24,16},{28,20},{1,9},{5... | collective-permute-start | bytes 884744 | tf_op jit(solution)/shard_map/ppermute | solution.py:860
  304.0 14.7 %collective-permute-done.22 = bf16[4,128,1152]{2,1,0:T(8,128)(2,1)S(1)} collective-permute-done((bf16[4,128,1152]{2,1,0:T(8,128)(2,1)S(1)}, bf16[4,128,1152]{2,1,0:T(8,128)(2,1)S(1)}, u32[]{:S(2)}, u32[]{:S(2)}) %collective-permute-start.22) | collective-permute-done | bytes 1179680 | tf_op jit(solution)/shard_map/ppermute | solution.py:860
  318.8 8.4 %collective-permute-start.29 = (bf16[128,1152]{1,0:T(8,128)(2,1)S(1)}, bf16[128,1152]{1,0:T(8,128)(2,1)S(1)}, u32[]{:S(2)}, u32[]{:S(2)}) collective-permute-start(bf16[128,1152]{1,0:T(8,128)(2,1)S(1)} %get-tuple-element.211), channel_id=1, source_target_pairs={{0,24},{4,28},{8,16},{12,20},{16,8},{20,12},{24,0},{28,4},{1,25},{... | collective-permute-start | bytes 884744 | tf_op jit(solution)/shard_map/ppermute | solution.py:860
  327.5 15.6 %collective-permute-done.30 = bf16[4,128,1152]{2,1,0:T(8,128)(2,1)S(1)} collective-permute-done((bf16[4,128,1152]{2,1,0:T(8,128)(2,1)S(1)}, bf16[4,128,1152]{2,1,0:T(8,128)(2,1)S(1)}, u32[]{:S(2)}, u32[]{:S(2)}) %collective-permute-start.30) | collective-permute-done | bytes 1179680 | tf_op jit(solution)/shard_map/ppermute | solution.py:860
  343.2 20.3 %collective-permute-start.28 = (bf16[128,1152]{1,0:T(8,128)(2,1)S(1)}, bf16[128,1152]{1,0:T(8,128)(2,1)S(1)}, u32[]{:S(2)}, u32[]{:S(2)}) collective-permute-start(bf16[128,1152]{1,0:T(8,128)(2,1)S(1)} %get-tuple-element.212), channel_id=1, source_target_pairs={{0,16},{4,20},{8,24},{12,28},{16,0},{20,4},{24,8},{28,12},{1,17},{... | collective-permute-start | bytes 884744 | tf_op jit(solution)/shard_map/ppermute | solution.py:860
  365.4 7.7 %collective-permute-done.28 = bf16[128,1152]{1,0:T(8,128)(2,1)S(1)} collective-permute-done((bf16[128,1152]{1,0:T(8,128)(2,1)S(1)}, bf16[128,1152]{1,0:T(8,128)(2,1)S(1)}, u32[]{:S(2)}, u32[]{:S(2)}) %collective-permute-start.28) | collective-permute-done | bytes 294944 | tf_op jit(solution)/shard_map/ppermute | solution.py:860
  374.5 8.0 %collective-permute-done.23 = bf16[128,1152]{1,0:T(8,128)(2,1)S(1)} collective-permute-done((bf16[128,1152]{1,0:T(8,128)(2,1)S(1)}, bf16[128,1152]{1,0:T(8,128)(2,1)S(1)}, u32[]{:S(2)}, u32[]{:S(2)}) %collective-permute-start.23) | collective-permute-done | bytes 294944 | tf_op jit(solution)/shard_map/ppermute | solution.py:860
  385.2 10.0 %collective-permute-done.24 = bf16[128,1152]{1,0:T(8,128)(2,1)S(1)} collective-permute-done((bf16[128,1152]{1,0:T(8,128)(2,1)S(1)}, bf16[128,1152]{1,0:T(8,128)(2,1)S(1)}, u32[]{:S(2)}, u32[]{:S(2)}) %collective-permute-start.24) | collective-permute-done | bytes 294944 | tf_op jit(solution)/shard_map/ppermute | solution.py:860
  397.3 2.3 collective-permute-start.33
  402.2 5.4 collective-permute-done.5
  407.6 1.9 fusion.43
  409.4 2.3 fusion.71
  413.3 12.8 %collective-permute-done.32 = bf16[128,1152]{1,0:T(8,128)(2,1)S(1)} collective-permute-done((bf16[128,1152]{1,0:T(8,128)(2,1)S(1)}, bf16[128,1152]{1,0:T(8,128)(2,1)S(1)}, u32[]{:S(2)}, u32[]{:S(2)}) %collective-permute-start.32) | collective-permute-done | bytes 294944 | tf_op jit(solution)/shard_map/ppermute | solution.py:860
  428.5 12.3 %collective-permute-done.14.refs_6_ = bf16[256,1024]{1,0:T(8,128)(2,1)S(1)} collective-permute-done((bf16[256,1024]{1,0:T(8,128)(2,1)}, bf16[256,1024]{1,0:T(8,128)(2,1)S(1)}, u32[]{:S(2)}, u32[]{:S(2)}) %collective-permute-start.14) | collective-permute-done | bytes 524320 | tf_op jit(solution)/shard_map/ppermute | solution.py:860
  441.8 29.6 %attention_backward.2 = (bf16[2,256,1024]{2,1,0:T(8,128)(2,1)}, bf16[2,256,1024]{2,1,0:T(8,128)(2,1)}, f32[8,128]{1,0:T(8,128)}, bf16[4,128,768]{2,1,0:T(8,128)(2,1)}, bf16[4,128,768]{2,1,0:T(8,128)(2,1)}) custom-call(s32[4]{0:T(128)} %pad_add_fusion.1.scal, f32[1024,128]{1,0:T(8,128)} %constant.101.clone.cos_ref, f32[1024,128]{1,0:T(8,128)} %constant.102.clone.sin_ref, ...), custom_call_target="tpu_custom_call" | custom-call | flops 14000000000 | bytes 15000000 | tf_op jit(solution)/shard_map/attention_backward/pallas_call | solution.py:374
  472.4 29.4 %attention_backward.3 = (bf16[2,256,1024]{2,1,0:T(8,128)(2,1)}, bf16[2,256,1024]{2,1,0:T(8,128)(2,1)}, f32[8,128]{1,0:T(8,128)}, bf16[4,128,768]{2,1,0:T(8,128)(2,1)}, bf16[4,128,768]{2,1,0:T(8,128)(2,1)}) custom-call(s32[4]{0:T(128)} %pad_add_fusion.scal, f32[1024,128]{1,0:T(8,128)} %constant.101.clone.cos_ref, f32[1024,128]{1,0:T(8,128)} %constant.102.clone.sin_ref, ...), custom_call_target="tpu_custom_call" | custom-call | flops 14000000000 | bytes 15000000 | tf_op jit(solution)/shard_map/attention_backward/pallas_call | solution.py:374
  505.5 2.1 collective-permute-done.40
  512.2 2.1 copy.41
  514.3 1.9 copy.40
  516.3 3.2 collective-permute-start.43
  519.6 2.0 copy.37
  522.3 5.7 collective-permute-done.18
  530.9 1.6 collective-permute-start.17
  533.4 2.7 collective-permute-start.21
  537.4 4.5 collective-permute-done.19
  541.9 3.1 collective-permute-done.21
  545.0 6.6 %collective-permute-done.20 = bf16[128,768]{1,0:T(8,128)(2,1)S(1)} collective-permute-done((bf16[128,768]{1,0:T(8,128)(2,1)S(1)}, bf16[128,768]{1,0:T(8,128)(2,1)S(1)}, u32[]{:S(2)}, u32[]{:S(2)}) %collective-permute-start.20) | collective-permute-done | bytes 196640 | tf_op jit(solution)/shard_map/ppermute | solution.py:860
  551.6 2.4 collective-permute-done.10
  554.1 2.3 fusion.9
  560.2 2.1 collective-permute-done.35
  563.6 2.3 collective-permute-done.36
  566.0 2.8 fusion.6
  569.6 2.5 collective-permute-start.38
  572.3 2.9 copy.38
  (271 shorter events, 85.6 us)
Async XLA Ops:
  194.1 101.9 %collective-permute-start.26 = (bf16[4,128,1152]{2,1,0:T(8,128)(2,1)}, bf16[4,128,1152]{2,1,0:T(8,128)(2,1)}, u32[]{:S(2)}, u32[]{:S(2)}) collective-permute-start(bf16[4,128,1152]{2,1,0:T(8,128)(2,1)} %get-tuple-element.90), channel_id=1, source_target_pairs={{0,4},{4,0},{8,12},{12,8},{16,20},{20,16},{24,28},{28,24},{1,5},{5... | collective-permute-start | bytes 3538952 | tf_op jit(solution)/shard_map/ppermute | solution.py:860
  255.0 34.9 %collective-permute-start.2 = (bf16[2,256,1024]{2,1,0:T(8,128)(2,1)}, bf16[2,256,1024]{2,1,0:T(8,128)(2,1)S(1)}, u32[]{:S(2)}, u32[]{:S(2)}) collective-permute-start(bf16[2,256,1024]{2,1,0:T(8,128)(2,1)} %get-tuple-element.66), channel_id=1, source_target_pairs={{0,1},{1,0},{2,3},{3,2},{4,5},{5,4},{6,7},{7,6},{8,9},{9,8},{10,11... | collective-permute-start | bytes 3145736 | tf_op jit(solution)/shard_map/ppermute | solution.py:860
  255.0 36.7 %collective-permute-start.11 = (bf16[2,256,1024]{2,1,0:T(8,128)(2,1)}, bf16[2,256,1024]{2,1,0:T(8,128)(2,1)S(1)}, u32[]{:S(2)}, u32[]{:S(2)}) collective-permute-start(bf16[2,256,1024]{2,1,0:T(8,128)(2,1)} %get-tuple-element.80), channel_id=1, source_target_pairs={{0,1},{1,0},{2,3},{3,2},{4,5},{5,4},{6,7},{7,6},{8,9},{9,8},{10,11... | collective-permute-start | bytes 3145736 | tf_op jit(solution)/shard_map/ppermute | solution.py:860
  271.3 21.1 %collective-permute-start = (bf16[2,256,1024]{2,1,0:T(8,128)(2,1)}, bf16[2,256,1024]{2,1,0:T(8,128)(2,1)S(1)}, u32[]{:S(2)}, u32[]{:S(2)}) collective-permute-start(bf16[2,256,1024]{2,1,0:T(8,128)(2,1)} %get-tuple-element.64), channel_id=1, source_target_pairs={{0,1},{1,0},{2,3},{3,2},{4,5},{5,4},{6,7},{7,6},{8,9},{9,8},{10,11... | collective-permute-start | bytes 3145736 | tf_op jit(solution)/shard_map/ppermute | solution.py:860
  271.5 24.2 %collective-permute-start.4 = (bf16[2,256,1024]{2,1,0:T(8,128)(2,1)}, bf16[2,256,1024]{2,1,0:T(8,128)(2,1)S(1)}, u32[]{:S(2)}, u32[]{:S(2)}) collective-permute-start(bf16[2,256,1024]{2,1,0:T(8,128)(2,1)} %get-tuple-element.68), channel_id=1, source_target_pairs={{0,1},{1,0},{2,3},{3,2},{4,5},{5,4},{6,7},{7,6},{8,9},{9,8},{10,11... | collective-permute-start | bytes 3145736 | tf_op jit(solution)/shard_map/ppermute | solution.py:860
  289.9 28.9 %collective-permute-start.22 = (bf16[4,128,1152]{2,1,0:T(8,128)(2,1)S(1)}, bf16[4,128,1152]{2,1,0:T(8,128)(2,1)S(1)}, u32[]{:S(2)}, u32[]{:S(2)}) collective-permute-start(bf16[4,128,1152]{2,1,0:T(8,128)(2,1)S(1)} %copy-done.44), channel_id=1, source_target_pairs={{0,4},{4,0},{8,12},{12,8},{16,20},{20,16},{24,28},{28,24},{1,5},{5... | collective-permute-start | bytes 3538952 | tf_op jit(solution)/shard_map/ppermute | solution.py:860
  291.8 51.4 %collective-permute-start.30 = (bf16[4,128,1152]{2,1,0:T(8,128)(2,1)S(1)}, bf16[4,128,1152]{2,1,0:T(8,128)(2,1)S(1)}, u32[]{:S(2)}, u32[]{:S(2)}) collective-permute-start(bf16[4,128,1152]{2,1,0:T(8,128)(2,1)S(1)} %copy-done.43), channel_id=1, source_target_pairs={{0,4},{4,0},{8,12},{12,8},{16,20},{20,16},{24,28},{28,24},{1,5},{5... | collective-permute-start | bytes 3538952 | tf_op jit(solution)/shard_map/ppermute | solution.py:860
  292.5 108.3 %collective-permute-start.3 = (bf16[256,1024]{1,0:T(8,128)(2,1)S(1)}, bf16[256,1024]{1,0:T(8,128)(2,1)S(1)}, u32[]{:S(2)}, u32[]{:S(2)}) collective-permute-start(bf16[256,1024]{1,0:T(8,128)(2,1)S(1)} %fusion.54), channel_id=1, source_target_pairs={{0,2},{1,3},{2,0},{3,1},{4,6},{5,7},{6,4},{7,5},{8,10},{9,11},{10,... | collective-permute-start | bytes 1572872 | tf_op jit(solution)/shard_map/ppermute | solution.py:860
  295.7 106.5 %collective-permute-start.12 = (bf16[256,1024]{1,0:T(8,128)(2,1)S(1)}, bf16[256,1024]{1,0:T(8,128)(2,1)S(1)}, u32[]{:S(2)}, u32[]{:S(2)}) collective-permute-start(bf16[256,1024]{1,0:T(8,128)(2,1)S(1)} %fusion.57), channel_id=1, source_target_pairs={{0,2},{1,3},{2,0},{3,1},{4,6},{5,7},{6,4},{7,5},{8,10},{9,11},{10,... | collective-permute-start | bytes 1572872 | tf_op jit(solution)/shard_map/ppermute | solution.py:860
  297.6 29.6 %copy-start.26 = (bf16[4,128,1152]{2,1,0:T(8,128)(2,1)S(1)}, bf16[4,128,1152]{2,1,0:T(8,128)(2,1)}, u32[]{:S(2)}) copy-start(bf16[4,128,1152]{2,1,0:T(8,128)(2,1)} %get-tuple-element.87) | copy-start | bytes 3538948
  297.6 66.2 %collective-permute-start.27 = (bf16[128,1152]{1,0:T(8,128)(2,1)S(1)}, bf16[128,1152]{1,0:T(8,128)(2,1)S(1)}, u32[]{:S(2)}, u32[]{:S(2)}) collective-permute-start(bf16[128,1152]{1,0:T(8,128)(2,1)S(1)} %get-tuple-element.210), channel_id=1, source_target_pairs={{0,8},{4,12},{8,0},{12,4},{16,24},{20,28},{24,16},{28,20},{1,9},{5... | collective-permute-start | bytes 884744 | tf_op jit(solution)/shard_map/ppermute | solution.py:860
  318.8 45.2 %collective-permute-start.29 = (bf16[128,1152]{1,0:T(8,128)(2,1)S(1)}, bf16[128,1152]{1,0:T(8,128)(2,1)S(1)}, u32[]{:S(2)}, u32[]{:S(2)}) collective-permute-start(bf16[128,1152]{1,0:T(8,128)(2,1)S(1)} %get-tuple-element.211), channel_id=1, source_target_pairs={{0,24},{4,28},{8,16},{12,20},{16,8},{20,12},{24,0},{28,4},{1,25},{... | collective-permute-start | bytes 884744 | tf_op jit(solution)/shard_map/ppermute | solution.py:860
  327.5 36.0 %copy-start.24 = (bf16[4,128,1152]{2,1,0:T(8,128)(2,1)S(1)}, bf16[4,128,1152]{2,1,0:T(8,128)(2,1)}, u32[]{:S(2)}) copy-start(bf16[4,128,1152]{2,1,0:T(8,128)(2,1)} %get-tuple-element.91) | copy-start | bytes 3538948
  343.2 29.9 %collective-permute-start.28 = (bf16[128,1152]{1,0:T(8,128)(2,1)S(1)}, bf16[128,1152]{1,0:T(8,128)(2,1)S(1)}, u32[]{:S(2)}, u32[]{:S(2)}) collective-permute-start(bf16[128,1152]{1,0:T(8,128)(2,1)S(1)} %get-tuple-element.212), channel_id=1, source_target_pairs={{0,16},{4,20},{8,24},{12,28},{16,0},{20,4},{24,8},{28,12},{1,17},{... | collective-permute-start | bytes 884744 | tf_op jit(solution)/shard_map/ppermute | solution.py:860
  363.9 18.6 %collective-permute-start.23 = (bf16[128,1152]{1,0:T(8,128)(2,1)S(1)}, bf16[128,1152]{1,0:T(8,128)(2,1)S(1)}, u32[]{:S(2)}, u32[]{:S(2)}) collective-permute-start(bf16[128,1152]{1,0:T(8,128)(2,1)S(1)} %get-tuple-element.207), channel_id=1, source_target_pairs={{0,8},{4,12},{8,0},{12,4},{16,24},{20,28},{24,16},{28,20},{1,9},{5... | collective-permute-start | bytes 884744 | tf_op jit(solution)/shard_map/ppermute | solution.py:860
  363.9 20.1 %collective-permute-start.25 = (bf16[128,1152]{1,0:T(8,128)(2,1)S(1)}, bf16[128,1152]{1,0:T(8,128)(2,1)S(1)}, u32[]{:S(2)}, u32[]{:S(2)}) collective-permute-start(bf16[128,1152]{1,0:T(8,128)(2,1)S(1)} %get-tuple-element.208), channel_id=1, source_target_pairs={{0,24},{4,28},{8,16},{12,20},{16,8},{20,12},{24,0},{28,4},{1,25},{... | collective-permute-start | bytes 884744 | tf_op jit(solution)/shard_map/ppermute | solution.py:860
  373.1 22.1 %collective-permute-start.24 = (bf16[128,1152]{1,0:T(8,128)(2,1)S(1)}, bf16[128,1152]{1,0:T(8,128)(2,1)S(1)}, u32[]{:S(2)}, u32[]{:S(2)}) collective-permute-start(bf16[128,1152]{1,0:T(8,128)(2,1)S(1)} %get-tuple-element.209), channel_id=1, source_target_pairs={{0,16},{4,20},{8,24},{12,28},{16,0},{20,4},{24,8},{28,12},{1,17},{... | collective-permute-start | bytes 884744 | tf_op jit(solution)/shard_map/ppermute | solution.py:860
  382.5 14.8 %collective-permute-start.1 = (bf16[256,1024]{1,0:T(8,128)(2,1)S(1)}, bf16[256,1024]{1,0:T(8,128)(2,1)S(1)}, u32[]{:S(2)}, u32[]{:S(2)}) collective-permute-start(bf16[256,1024]{1,0:T(8,128)(2,1)S(1)} %fusion.53), channel_id=1, source_target_pairs={{0,2},{1,3},{2,0},{3,1},{4,6},{5,7},{6,4},{7,5},{8,10},{9,11},{10,... | collective-permute-start | bytes 1572872 | tf_op jit(solution)/shard_map/ppermute | solution.py:860
  384.0 23.6 %collective-permute-start.5 = (bf16[256,1024]{1,0:T(8,128)(2,1)S(1)}, bf16[256,1024]{1,0:T(8,128)(2,1)S(1)}, u32[]{:S(2)}, u32[]{:S(2)}) collective-permute-start(bf16[256,1024]{1,0:T(8,128)(2,1)S(1)} %fusion.55), channel_id=1, source_target_pairs={{0,2},{1,3},{2,0},{3,1},{4,6},{5,7},{6,4},{7,5},{8,10},{9,11},{10,... | collective-permute-start | bytes 1572872 | tf_op jit(solution)/shard_map/ppermute | solution.py:860
  395.2 18.1 %collective-permute-start.31 = (bf16[128,1152]{1,0:T(8,128)(2,1)S(1)}, bf16[128,1152]{1,0:T(8,128)(2,1)S(1)}, u32[]{:S(2)}, u32[]{:S(2)}) collective-permute-start(bf16[128,1152]{1,0:T(8,128)(2,1)S(1)} %get-tuple-element.213), channel_id=1, source_target_pairs={{0,8},{4,12},{8,0},{12,4},{16,24},{20,28},{24,16},{28,20},{1,9},{5... | collective-permute-start | bytes 884744 | tf_op jit(solution)/shard_map/ppermute | solution.py:860
  397.3 16.0 %collective-permute-start.33 = (bf16[128,1152]{1,0:T(8,128)(2,1)S(1)}, bf16[128,1152]{1,0:T(8,128)(2,1)S(1)}, u32[]{:S(2)}, u32[]{:S(2)}) collective-permute-start(bf16[128,1152]{1,0:T(8,128)(2,1)S(1)} %get-tuple-element.214), channel_id=1, source_target_pairs={{0,24},{4,28},{8,16},{12,20},{16,8},{20,12},{24,0},{28,4},{1,25},{... | collective-permute-start | bytes 884744 | tf_op jit(solution)/shard_map/ppermute | solution.py:860
  400.8 25.2 %collective-permute-start.32 = (bf16[128,1152]{1,0:T(8,128)(2,1)S(1)}, bf16[128,1152]{1,0:T(8,128)(2,1)S(1)}, u32[]{:S(2)}, u32[]{:S(2)}) collective-permute-start(bf16[128,1152]{1,0:T(8,128)(2,1)S(1)} %get-tuple-element.215), channel_id=1, source_target_pairs={{0,16},{4,20},{8,24},{12,28},{16,0},{20,4},{24,8},{28,12},{1,17},{... | collective-permute-start | bytes 884744 | tf_op jit(solution)/shard_map/ppermute | solution.py:860
  411.7 16.1 %collective-permute-start.7 = (bf16[256,1024]{1,0:T(8,128)(2,1)S(1)}, bf16[256,1024]{1,0:T(8,128)(2,1)S(1)}, u32[]{:S(2)}, u32[]{:S(2)}) collective-permute-start(bf16[256,1024]{1,0:T(8,128)(2,1)S(1)} %get-tuple-element.120.refs_4_), channel_id=1, source_target_pairs={{0,2},{1,3},{2,0},{3,1},{4,6},{5,7},{6,4},{7,5},{8,10},{9,11},{10,... | collective-permute-start | bytes 1572872 | tf_op jit(solution)/shard_map/ppermute | solution.py:860
  426.1 14.6 %collective-permute-start.6 = (bf16[256,1024]{1,0:T(8,128)(2,1)S(1)}, bf16[256,1024]{1,0:T(8,128)(2,1)S(1)}, u32[]{:S(2)}, u32[]{:S(2)}) collective-permute-start(bf16[256,1024]{1,0:T(8,128)(2,1)S(1)} %get-tuple-element.120.refs_4_), channel_id=1, source_target_pairs={{0,1},{1,0},{2,3},{3,2},{4,5},{5,4},{6,7},{7,6},{8,9},{9,8},{10,11... | collective-permute-start | bytes 1572872 | tf_op jit(solution)/shard_map/ppermute | solution.py:860
  426.2 14.6 %collective-permute-start.14 = (bf16[256,1024]{1,0:T(8,128)(2,1)}, bf16[256,1024]{1,0:T(8,128)(2,1)S(1)}, u32[]{:S(2)}, u32[]{:S(2)}) collective-permute-start(bf16[256,1024]{1,0:T(8,128)(2,1)} %get-tuple-element.169.refs_4_), channel_id=1, source_target_pairs={{0,2},{1,3},{2,0},{3,1},{4,6},{5,7},{6,4},{7,5},{8,10},{9,11},{10,... | collective-permute-start | bytes 1572872 | tf_op jit(solution)/shard_map/ppermute | solution.py:860
  427.8 13.0 %collective-permute-start.8 = (bf16[256,1024]{1,0:T(8,128)(2,1)S(1)}, bf16[256,1024]{1,0:T(8,128)(2,1)S(1)}, u32[]{:S(2)}, u32[]{:S(2)}) collective-permute-start(bf16[256,1024]{1,0:T(8,128)(2,1)S(1)} %collective-permute-done.7.refs_6_), channel_id=1, source_target_pairs={{0,1},{1,0},{2,3},{3,2},{4,5},{5,4},{6,7},{7,6},{8,9},{9,8},{10,11... | collective-permute-start | bytes 1572872 | tf_op jit(solution)/shard_map/ppermute | solution.py:860
  428.1 43.3 %collective-permute-start.13 = (bf16[256,1024]{1,0:T(8,128)(2,1)}, bf16[256,1024]{1,0:T(8,128)(2,1)S(1)}, u32[]{:S(2)}, u32[]{:S(2)}) collective-permute-start(bf16[256,1024]{1,0:T(8,128)(2,1)} %get-tuple-element.169.refs_4_), channel_id=1, source_target_pairs={{0,1},{1,0},{2,3},{3,2},{4,5},{5,4},{6,7},{7,6},{8,9},{9,8},{10,11... | collective-permute-start | bytes 1572872 | tf_op jit(solution)/shard_map/ppermute | solution.py:860
  440.8 30.6 %copy-start.46 = (bf16[256,1024]{1,0:T(8,128)(2,1)}, bf16[256,1024]{1,0:T(8,128)(2,1)S(1)}, u32[]{:S(2)}) copy-start(bf16[256,1024]{1,0:T(8,128)(2,1)S(1)} %collective-permute-done.14.refs_6_) | copy-start | bytes 1572868
  440.8 30.6 %collective-permute-start.15 = (bf16[256,1024]{1,0:T(8,128)(2,1)S(1)}, bf16[256,1024]{1,0:T(8,128)(2,1)S(1)}, u32[]{:S(2)}, u32[]{:S(2)}) collective-permute-start(bf16[256,1024]{1,0:T(8,128)(2,1)S(1)} %collective-permute-done.14.refs_6_), channel_id=1, source_target_pairs={{0,1},{1,0},{2,3},{3,2},{4,5},{5,4},{6,7},{7,6},{8,9},{9,8},{10,11... | collective-permute-start | bytes 1572872 | tf_op jit(solution)/shard_map/ppermute | solution.py:860
  472.4 29.4 %copy-start.42 = (f32[8,128]{1,0:T(8,128)S(1)}, f32[8,128]{1,0:T(8,128)}, u32[]{:S(2)}) copy-start(f32[8,128]{1,0:T(8,128)} %get-tuple-element.93) | copy-start | bytes 12292
  502.6 1.3 collective-permute-start.39
  503.9 3.7 collective-permute-start.40
  507.6 3.7 collective-permute-start.41
  509.2 18.8 %collective-permute-start.18 = (bf16[4,128,768]{2,1,0:T(8,128)(2,1)}, bf16[4,128,768]{2,1,0:T(8,128)(2,1)}, u32[]{:S(2)}, u32[]{:S(2)}) collective-permute-start(bf16[4,128,768]{2,1,0:T(8,128)(2,1)} %add_convert_fusion), channel_id=1, source_target_pairs={{0,4},{4,0},{8,12},{12,8},{16,20},{20,16},{24,28},{28,24},{1,5},{5... | collective-permute-start | bytes 2359304 | tf_op jit(solution)/shard_map/ppermute | solution.py:860
  510.7 18.9 %collective-permute-start.16 = (bf16[2,256,1024]{2,1,0:T(8,128)(2,1)}, bf16[2,256,1024]{2,1,0:T(8,128)(2,1)}, u32[]{:S(2)}, u32[]{:S(2)}) collective-permute-start(bf16[2,256,1024]{2,1,0:T(8,128)(2,1)} %get-tuple-element.82), channel_id=1, source_target_pairs={{0,1},{1,0},{2,3},{3,2},{4,5},{5,4},{6,7},{7,6},{8,9},{9,8},{10,11... | collective-permute-start | bytes 3145736 | tf_op jit(solution)/shard_map/ppermute | solution.py:860
  511.3 4.9 collective-permute-start.42
  516.3 5.4 collective-permute-start.43
  521.6 10.8 %collective-permute-start.9 = (bf16[2,256,1024]{2,1,0:T(8,128)(2,1)S(1)}, bf16[2,256,1024]{2,1,0:T(8,128)(2,1)S(1)}, u32[]{:S(2)}, u32[]{:S(2)}) collective-permute-start(bf16[2,256,1024]{2,1,0:T(8,128)(2,1)S(1)} %copy-done.45), channel_id=1, source_target_pairs={{0,1},{1,0},{2,3},{3,2},{4,5},{5,4},{6,7},{7,6},{8,9},{9,8},{10,11... | collective-permute-start | bytes 3145736 | tf_op jit(solution)/shard_map/ppermute | solution.py:860
  530.9 20.7 %collective-permute-start.17 = (bf16[256,1024]{1,0:T(8,128)(2,1)S(1)}, bf16[256,1024]{1,0:T(8,128)(2,1)S(1)}, u32[]{:S(2)}, u32[]{:S(2)}) collective-permute-start(bf16[256,1024]{1,0:T(8,128)(2,1)S(1)} %fusion.58), channel_id=1, source_target_pairs={{0,2},{1,3},{2,0},{3,1},{4,6},{5,7},{6,4},{7,5},{8,10},{9,11},{10,... | collective-permute-start | bytes 1572872 | tf_op jit(solution)/shard_map/ppermute | solution.py:860
  532.7 21.4 %collective-permute-start.10 = (bf16[256,1024]{1,0:T(8,128)(2,1)S(1)}, bf16[256,1024]{1,0:T(8,128)(2,1)S(1)}, u32[]{:S(2)}, u32[]{:S(2)}) collective-permute-start(bf16[256,1024]{1,0:T(8,128)(2,1)S(1)} %fusion.56), channel_id=1, source_target_pairs={{0,2},{1,3},{2,0},{3,1},{4,6},{5,7},{6,4},{7,5},{8,10},{9,11},{10,... | collective-permute-start | bytes 1572872 | tf_op jit(solution)/shard_map/ppermute | solution.py:860
  533.3 8.6 %collective-permute-start.19 = (bf16[128,768]{1,0:T(8,128)(2,1)S(1)}, bf16[128,768]{1,0:T(8,128)(2,1)S(1)}, u32[]{:S(2)}, u32[]{:S(2)}) collective-permute-start(bf16[128,768]{1,0:T(8,128)(2,1)S(1)} %get-tuple-element.224), channel_id=1, source_target_pairs={{0,8},{4,12},{8,0},{12,4},{16,24},{20,28},{24,16},{28,20},{1,9},{5... | collective-permute-start | bytes 589832 | tf_op jit(solution)/shard_map/ppermute | solution.py:860
  533.4 11.6 %collective-permute-start.21 = (bf16[128,768]{1,0:T(8,128)(2,1)S(1)}, bf16[128,768]{1,0:T(8,128)(2,1)S(1)}, u32[]{:S(2)}, u32[]{:S(2)}) collective-permute-start(bf16[128,768]{1,0:T(8,128)(2,1)S(1)} %get-tuple-element.225), channel_id=1, source_target_pairs={{0,24},{4,28},{8,16},{12,20},{16,8},{20,12},{24,0},{28,4},{1,25},{... | collective-permute-start | bytes 589832 | tf_op jit(solution)/shard_map/ppermute | solution.py:860
  536.1 15.4 %collective-permute-start.20 = (bf16[128,768]{1,0:T(8,128)(2,1)S(1)}, bf16[128,768]{1,0:T(8,128)(2,1)S(1)}, u32[]{:S(2)}, u32[]{:S(2)}) collective-permute-start(bf16[128,768]{1,0:T(8,128)(2,1)S(1)} %get-tuple-element.226), channel_id=1, source_target_pairs={{0,16},{4,20},{8,24},{12,28},{16,0},{20,4},{24,8},{28,12},{1,17},{... | collective-permute-start | bytes 589832 | tf_op jit(solution)/shard_map/ppermute | solution.py:860
  556.5 2.2 collective-permute-start.34
  558.7 3.6 collective-permute-start.35
  562.3 3.6 collective-permute-start.36
  565.9 3.6 collective-permute-start.37
  569.6 5.7 collective-permute-start.38
  (50 other events, 282.6 us)
